TPU v7x, 32 devices: a whole 2x2x4 slice. The times are simulated.
32 devices in a mesh: ctx: 8 (over y, x, core), tp: 4 (over z).
Axes of the slice: x: 2, y: 2, z: 4, core: 2. Of those that a mesh axis runs over, the one named last changes fastest.
Arguments:
- ssm_input: bfloat16 [2048, 4096], P('ctx', 'tp'), may hold values from -6 to 6
- dt_raw: float32 [2048, 64], P('ctx', 'tp'), may hold values from -5 to 5
- b_proj: bfloat16 [2048, 4, 256], P('ctx', 'tp'), may hold values from -0.59765625 to 0.59765625
- c_proj: bfloat16 [2048, 4, 256], P('ctx', 'tp'), may hold values from -0.59765625 to 0.59765625
- dt_bias: float32 [64], P('tp'), may hold values from -1.5 to 0.5
- decay_rate: float32 [64], P('tp'), may hold values from 0.0002 to 0.05
- skip_gain: float32 [64], P('tp'), may hold values from 0.5 to 1.5
- doc_start: int32 [2048], P('ctx'), may hold values 0 or 1
- out_weight: bfloat16 [4096, 8192], P('tp'), may hold values from -0.09375 to 0.09375
- grad_out: bfloat16 [2048, 8192], P(('ctx', 'tp')), may hold values from -6 to 6
Outputs:
- layer_out: bfloat16 [2048, 8192], P(('ctx', 'tp'))
- grad_input: bfloat16 [2048, 4096], P('ctx', 'tp')
- grad_dt: float32 [2048, 64], P('ctx', 'tp')
- grad_b: bfloat16 [2048, 4, 256], P('ctx', 'tp')
- grad_c: bfloat16 [2048, 4, 256], P('ctx', 'tp')
- weight_grad: bfloat16 [8192, 4096], P('ctx', 'tp')
Inputs may be any that keep to these rules, and one draw needn't show every extreme that they name: `doc_start`: 1 marks the first token of a document; a document runs on until the next 1, across slabs.
All inputs are finite; a program needn't handle non-finite values. No bound on the sum of `doc_start` on one device may be relied on, other than what follows from the above.
Results may differ from a plain program's by a relative error of at most 0.022.
Values may be sent and summed in bfloat16 or wider, within the bound.
A program may use at most 256 MiB of HBM per device.

v0:
```python
import jax
import jax.numpy as jnp
from jax import lax
from jax.sharding import PartitionSpec as P

HIGHEST = lax.Precision.HIGHEST


def prefix(value, axis, combine, identity, reverse):
    devices, mine = (lax.axis_size(axis), lax.axis_index(axis))
    everything = jax.tree.map(
        lambda part, kind: lax.all_gather(part.astype(kind), axis),
        value,
        (jnp.bfloat16, jnp.bfloat16),
    )
    start = jax.tree.map(
        lambda part, zero: jnp.broadcast_to(jnp.asarray(zero, part.dtype), part.shape),
        value,
        identity,
    )

    def step(k, before):
        at = devices - 1 - k if reverse else k
        reached = at > mine if reverse else at < mine
        new = combine(
            before, jax.tree.map(lambda part, own: part[at].astype(own.dtype), everything, value)
        )
        return jax.tree.map(lambda a, b: jnp.where(reached, a, b), new, before)

    return lax.fori_loop(0, devices, step, start)


def block_ssd(
    seq_in, step_raw, b_rows, c_rows, scores, carried, doc_start, bias_heads, rate_heads, skip_heads
):
    length = seq_in.shape[0]
    step_size = jax.nn.softplus(step_raw + bias_heads)
    cumul = jnp.cumsum(-step_size * rate_heads, axis=0)
    segment = jnp.cumsum(doc_start)
    reach = (segment == 0).astype(jnp.float32)
    order = jnp.arange(length)
    causal = (segment[:, None] == segment[None, :]) & (order[:, None] >= order[None, :])
    cum_heads = jnp.transpose(cumul, (1, 2, 0))
    differ = cum_heads[:, :, :, None] - cum_heads[:, :, None, :]
    decays = jnp.exp(jnp.where(causal, differ, -jnp.inf))
    mixing = decays * scores[:, None] * jnp.transpose(step_size, (1, 2, 0))[:, :, None, :]
    inside = jnp.einsum("gkts,sgkp->tgkp", mixing, seq_in, precision=HIGHEST)
    entry = jnp.exp(cumul) * reach[:, None, None]
    from_carry = entry[..., None] * jnp.einsum("tgn,gkpn->tgkp", c_rows, carried, precision=HIGHEST)
    mixer = inside + from_carry + skip_heads[..., None] * seq_in
    same_last = (segment == segment[-1]).astype(jnp.float32)
    tail = jnp.exp(cumul[-1] - cumul) * same_last[:, None, None] * step_size
    local_state = jnp.einsum("sgk,sgkp,sgn->gkpn", tail, seq_in, b_rows, precision=HIGHEST)
    through = reach[-1] * jnp.exp(cumul[-1])
    return (mixer, local_state, through)


def chain_combine(earlier, later):
    return (earlier[0] * later[0], later[0][..., None, None] * earlier[1] + later[1])


def shards(
    ssm_input,
    dt_raw,
    b_proj,
    c_proj,
    dt_bias,
    decay_rate,
    skip_gain,
    doc_start,
    out_weight,
    grad_out,
):
    rows = ssm_input.shape[0]
    heads = dt_raw.shape[1]
    head_dim = ssm_input.shape[1] // heads
    seq_f32 = ssm_input.astype(jnp.float32).reshape(rows, 1, heads, head_dim)
    step_raw = dt_raw.reshape(rows, 1, heads)
    b_rows = b_proj.astype(jnp.float32)
    c_rows = c_proj.astype(jnp.float32)
    bias_heads = dt_bias.reshape(1, heads)
    rate_heads = decay_rate.reshape(1, heads)
    skip_heads = skip_gain.reshape(1, heads)
    scores = jnp.einsum("tgn,sgn->gts", c_proj, b_proj, preferred_element_type=jnp.float32)
    step_size = jax.nn.softplus(step_raw + bias_heads)
    cumul = jnp.cumsum(-step_size * rate_heads, axis=0)
    segment = jnp.cumsum(doc_start)
    reach = (segment == 0).astype(jnp.float32)
    same_last = (segment == segment[-1]).astype(jnp.float32)
    tail = jnp.exp(cumul[-1] - cumul) * same_last[:, None, None] * step_size
    local_state = jnp.einsum("sgk,sgkp,sgn->gkpn", tail, seq_f32, b_rows, precision=HIGHEST)
    through = reach[-1] * jnp.exp(cumul[-1])
    identity_pair = (jnp.ones_like(through), jnp.zeros_like(local_state))
    carried = prefix((through, local_state), "ctx", chain_combine, identity_pair, False)[1]

    def local_fn(seq_arg, step_arg, b_arg, c_arg, score_arg):
        return block_ssd(
            seq_arg,
            step_arg,
            b_arg,
            c_arg,
            score_arg,
            carried,
            doc_start,
            bias_heads,
            rate_heads,
            skip_heads,
        )

    (mixer, _, _), pullback = jax.vjp(local_fn, seq_f32, step_raw, b_rows, c_rows, scores)
    mixer_bf = mixer.reshape(rows, heads * head_dim).astype(jnp.bfloat16)
    layer_out = lax.psum_scatter(
        jnp.dot(mixer_bf, out_weight, preferred_element_type=jnp.float32).astype(jnp.bfloat16),
        "tp",
        scatter_dimension=0,
        tiled=True,
    )
    grad_full = lax.all_gather(grad_out, "tp", axis=0, tiled=True)
    grad_mix = lax.dot_general(
        grad_full, out_weight, (((1,), (1,)), ((), ())), preferred_element_type=jnp.float32
    ).astype(jnp.bfloat16)
    grad_heads = grad_mix.astype(jnp.float32).reshape(rows, 1, heads, head_dim)
    entry = jnp.exp(cumul) * reach[:, None, None]
    local_grad = jnp.einsum("tgk,tgkp,tgn->gkpn", entry, grad_heads, c_rows, precision=HIGHEST)
    grad_next = prefix((through, local_grad), "ctx", chain_combine, identity_pair, True)[1]
    through_grad = jnp.sum(grad_next * carried, axis=(2, 3))
    grad_seq, grad_step, grad_brows, grad_crows, grad_scores = pullback(
        (grad_heads, grad_next, through_grad)
    )
    grad_brows = grad_brows + jnp.einsum("gts,tgn->sgn", grad_scores, c_rows, precision=HIGHEST)
    grad_crows = grad_crows + jnp.einsum("gts,sgn->tgn", grad_scores, b_rows, precision=HIGHEST)
    weight_sum = lax.psum_scatter(
        lax.dot_general(
            grad_full, mixer_bf, (((0,), (0,)), ((), ())), preferred_element_type=jnp.float32
        ).astype(jnp.bfloat16),
        "ctx",
        scatter_dimension=0,
        tiled=True,
    )
    return (
        layer_out,
        grad_seq.reshape(rows, heads * head_dim).astype(jnp.bfloat16),
        grad_step.reshape(rows, heads),
        grad_brows.astype(jnp.bfloat16),
        grad_crows.astype(jnp.bfloat16),
        weight_sum,
    )


def solution(mesh):
    in_specs = (
        P("ctx", "tp"),
        P("ctx", "tp"),
        P("ctx", "tp", None),
        P("ctx", "tp", None),
        P("tp"),
        P("tp"),
        P("tp"),
        P("ctx"),
        P("tp", None),
        P(("ctx", "tp"), None),
    )
    out_specs = (
        P(("ctx", "tp"), None),
        P("ctx", "tp"),
        P("ctx", "tp"),
        P("ctx", "tp", None),
        P("ctx", "tp", None),
        P("ctx", "tp"),
    )
    return jax.shard_map(shards, mesh=mesh, in_specs=in_specs, out_specs=out_specs, check_vma=False)
```

profile of v0, /device:TPU:0, one launch (start us, length us, event | category | flops | bytes accessed | tf_op | source)
XLA Modules:
  0.0 445.5 jit_solution(10249947561227269690)
XLA Ops:
  12.2 80.8 %all-gather.6.cloned.1.call-done = bf16[256,8192]{1,0:T(8,128)(2,1)} async-done(((bf16[64,8192]{1,0:T(8,128)(2,1)}), bf16[256,8192]{1,0:T(8,128)(2,1)}) %all-gather.6.cloned.1.call-update) | async-done | bytes 4194320 | tf_op jit(solution)/shard_map/all_gather | solution.py:118
  93.1 11.6 %convolution_convert_fusion.3 = bf16[256,1024]{1,0:T(8,128)(2,1)S(1)} fusion(bf16[256,8192]{1,0:T(8,128)(2,1)} %all-gather.6.cloned.1.call-done, bf16[1024,8192]{1,0:T(8,128)(2,1)} %param.22), kind=kOutput, calls=%fused_computation.43 | convolution fusion | flops 4295229440 | bytes 21495808 | tf_op jit(solution)/shard_map/dot_general | solution.py:119
  109.0 9.4 %all_gather.21 = bf16[8,1,16]{2,1,0:T(2,128)(2,1)} all-gather(bf16[1,1,16]{2,1,0:T(2,128)(2,1)S(1)} %get-tuple-element.399), channel_id=1, replica_groups=mesh['ctx'=8,'tp'=4] {'ctx'}, dimensions={0}, use_global_device_ids=true | all-gather | bytes 288 | tf_op jit(solution)/shard_map/all_gather | solution.py:12
  118.4 1.9 compare_convert_fusion
  120.3 21.5 %all-gather.10.cloned.1.call-done = bf16[128,64,256]{2,1,0:T(8,128)(2,1)} async-done(((bf16[16,64,256]{2,1,0:T(8,128)(2,1)}), bf16[128,64,256]{2,1,0:T(8,128)(2,1)}) %all-gather.10.cloned.1.call-update) | async-done | bytes 4194320 | tf_op jit(solution)/shard_map/all_gather | solution.py:12
  141.8 15.7 %while.31 = (s32[]{:T(128)}, f32[1,16,64,256]{3,2,1,0:T(8,128)S(1)}, s32[]{:T(128)}, bf16[8,1,16]{2,1,0:T(2,128)(2,1)}, bf16[8,1,16,64,256]{4,3,2,1,0:T(8,128)(2...) while((s32[]{:T(128)}, f32[1,16,64,256]{3,2,1,0:T(8,128)S(1)}, s32[]{:T(128)}, ...), condition=%wide.region_8.9_spmd.clone, body=%wide.region_7.8_spmd.clone.sunk | while | flops 1310744 | bytes 2621775 | solution.py:30
  157.5 2.2 fusion.50
  161.2 1.6 multiply_multiply_fusion
  163.5 1.7 multiply_reduce_fusion.4
  167.3 1.6 copy.146
  168.9 2.2 convolution_convert_fusion.2
  177.8 1.6 copy.140
  179.4 28.6 %all-gather.8.cloned.1.call-done = bf16[128,64,256]{2,1,0:T(8,128)(2,1)} async-done(((bf16[16,64,256]{2,1,0:T(8,128)(2,1)}), bf16[128,64,256]{2,1,0:T(8,128)(2,1)}) %all-gather.8.cloned.1.call-update) | async-done | bytes 4194320 | tf_op jit(solution)/shard_map/all_gather | solution.py:12
  208.0 15.7 %while.30 = (s32[]{:T(128)}, f32[1,16,64,256]{3,2,1,0:T(8,128)S(1)}, s32[]{:T(128)}, bf16[8,1,16]{2,1,0:T(2,128)(2,1)}, bf16[8,1,16,64,256]{4,3,2,1,0:T(8,128)(2,1)}, /*index=5*/s32[]{:T(128)}, s32[]{:T(128)}) while((s32[]{:T(128)}, f32[1,16,64,256]{3,2,1,0:T(8,128)S(1)}, s32[]{:T(128)}, bf16[8,1,16]{2,1,0:T(2,128)(2,1)}, ...), condition=%wide.region_5.6_spmd.clone, body=%wide.region_4.5_spmd.clone.sunk | while | flops 1310740 | bytes 2621713 | solution.py:30
  224.9 5.8 %fusion.40 = bf16[256,1,16,64]{0,3,2,1:T(8,128)(2,1)} fusion(bf16[256,16,64]{0,2,1:T(8,128)(2,1)} %bitcast.245, f32[16,256]{1,0:T(8,128)} %copy.140, f32[256,256]{1,0:T(8,128)} %fusion.77, f32[16,256]{1,0:T(8,128)} %bitcast_add_fusion.2, pred[256,256]{1,0:T(8,128)(4,1)} %fusion.62, f32[256,1,16,64]{0,3,2,1:T(8,128)} %bitcast.258, ...), kind=kOutput, calls=%fused_computation.42 | convolution fusion | flops 810811392 | bytes 3522624 | tf_op jit(solution)/shard_map/jvp(gkts,sgkp->tgkp)/dot_general | solution.py:47
  230.7 12.6 %convert_bitcast_fusion = bf16[8192,1024]{0,1:T(8,128)(2,1)} fusion(bf16[256,1024]{0,1:T(8,128)(2,1)} %bitcast.248, bf16[256,8192]{1,0:T(8,128)(2,1)} %all-gather.6.cloned.1.call-done), kind=kOutput, calls=%fused_computation.6 | convolution fusion | flops 4303355904 | bytes 21495808 | tf_op jit(solution)/shard_map/dot_general | solution.py:133
  243.6 13.4 %convolution_convert_fusion = bf16[256,8192]{1,0:T(8,128)(2,1)} fusion(bf16[256,1024]{0,1:T(8,128)(2,1)} %bitcast.249, bf16[1024,8192]{1,0:T(8,128)(2,1)} %param.22), kind=kOutput, calls=%fused_computation.7 | convolution fusion | flops 4297064448 | bytes 21495808 | tf_op jit(solution)/shard_map/dot_general | solution.py:113
  257.1 2.1 copy.152
  259.2 5.6 %fusion.37 = bf16[256,1,16,64]{0,3,2,1:T(8,128)(2,1)} fusion(bf16[16,64,256]{2,1,0:T(8,128)(2,1)} %bitcast.260, f32[16,256]{1,0:T(8,128)} %copy.140, f32[256,256]{1,0:T(8,128)} %fusion.77, f32[16,256]{1,0:T(8,128)} %bitcast_add_fusion.2, pred[256,256]{1,0:T(8,128)(4,1)} %fusion.62, f32[256,16,64]{0,2,1:T(8,128)S(1)} %bitcast.242, ...), kind=kOutput, calls=%fused_computation.39 | convolution fusion | flops 810811392 | bytes 3522624 | tf_op jit(solution)/shard_map/transpose(jvp(gkts,sgkp->tgkp))/dot_general | solution.py:47
  264.8 2.2 copy.162
  267.0 5.5 %fusion.9 = (f32[16,256]{1,0:T(8,128)}, f32[16,256]{1,0:T(8,128)}, f32[16,256]{1,0:T(8,128)}, f32[256,256]{1,0:T(8,128)}) fusion(f32[16,256]{1,0:T(8,128)} %copy.140, f32[256,256]{1,0:T(8,128)} %fusion.77, f32[16,256]{1,0:T(8,128)} %bitcast_add_fusion.2, pred[256,256]{1,0:T(8,128)(4,1)} %fusion.62, bf16[16,64,256]{2,1,0:T(8,128)(2,1)} %bitcast.261, ...), kind=kOutput, calls=%fused_computation.17 | convolution fusion | flops 147771392 | bytes 1720320 | tf_op jit(solution)/shard_map/transpose(jvp(gkts,sgkp->tgkp))/dot_general | solution.py:47
  276.8 2.9 fusion.44
  279.7 1.9 fusion.49
  281.6 1.7 copy.164
  283.3 1.9 convolution_bitcast_fusion.2
  286.2 1.5 copy.155
  289.2 1.5 add_add_fusion
  290.7 2.5 reduce-window.29
  295.4 3.4 fusion.47
  298.8 60.7 %reduce-scatter.5.cloned.1.call-done = bf16[1024,1024]{0,1:T(8,128)(2,1)} async-done(((bf16[8192,1024]{0,1:T(8,128)(2,1)}), bf16[1024,1024]{0,1:T(8,128)(2,1)}) %reduce-scatter.5.cloned.1.call-update) | async-done | bytes 2097168 | tf_op jit(solution)/shard_map/reduce_scatter | solution.py:132
  359.5 3.9 copy.165
  363.4 75.6 %reduce-scatter.3.cloned.1.call-done = bf16[64,8192]{1,0:T(8,128)(2,1)} async-done(((bf16[256,8192]{1,0:T(8,128)(2,1)}), bf16[64,8192]{1,0:T(8,128)(2,1)}) %reduce-scatter.3.cloned.1.call-update) | async-done | bytes 1048592 | tf_op jit(solution)/shard_map/reduce_scatter | solution.py:112
  (117 shorter events, 61.8 us)
Async XLA Ops:
  7.2 97.7 %copy-start = (bf16[256,1,256]{2,0,1:T(8,128)(2,1)S(1)}, bf16[256,1,256]{2,0,1:T(8,128)(2,1)}, u32[]{:S(2)}) copy-start(bf16[256,1,256]{2,0,1:T(8,128)(2,1)} %param.17) | copy-start | bytes 393220
  7.2 85.9 %all-gather.6.cloned.1.call-start = ((), (), s32[]{:S(2)}) async-start(), calls=%async_computation.3 | async-start | bytes 5242880 | tf_op jit(solution)/shard_map/all_gather | solution.py:118
  7.9 133.9 %all-gather.10.cloned.1.call-start = ((), (), s32[]{:S(2)}) async-start(), calls=%async_computation.6 | async-start | bytes 4718592 | tf_op jit(solution)/shard_map/all_gather | solution.py:12
  11.8 94.6 %copy-start.12 = (f32[256]{0:T(256)}, f32[256]{0:T(256)S(1)}, u32[]{:S(2)}) copy-start(f32[256]{0:T(256)S(1)} %get-tuple-element.392) | copy-start | bytes 3076
  11.8 95.3 %copy-start.11 = (s32[256]{0:T(256)}, s32[256]{0:T(256)S(1)}, u32[]{:S(2)}) copy-start(s32[256]{0:T(256)S(1)} %get-tuple-element.393) | copy-start | bytes 3076
  11.8 81.3 %copy-start.8 = (f32[16,2,128]{0,2,1:T(8,128)}, f32[16,2,128]{0,2,1:T(8,128)S(1)}, u32[]{:S(2)}) copy-start(f32[16,2,128]{0,2,1:T(8,128)S(1)} %broadcast.148) | copy-start | bytes 49156
  12.2 95.7 %copy-start.5 = (f32[256,1,16]{2,1,0:T(1,128)}, f32[256,1,16]{2,1,0:T(1,128)S(1)}, u32[]{:S(2)}) copy-start(f32[256,1,16]{2,1,0:T(1,128)S(1)} %get-tuple-element.391) | copy-start | bytes 49156
  12.2 92.6 %copy-start.9 = (f32[256,16]{0,1:T(8,128)}, f32[256,16]{0,1:T(8,128)S(1)}, u32[]{:S(2)}) copy-start(f32[256,16]{0,1:T(8,128)S(1)} %copy.144) | copy-start | bytes 49156
  104.7 1.8 copy-start.3
  104.7 3.0 copy-start.2
  106.4 101.6 %all-gather.8.cloned.1.call-start = ((), (), s32[]{:S(2)}) async-start(), calls=%async_computation.5 | async-start | bytes 4718592 | tf_op jit(solution)/shard_map/all_gather | solution.py:12
  107.8 61.1 %copy-start.1 = (bf16[256,1024]{0,1:T(8,128)(2,1)}, bf16[256,1024]{0,1:T(8,128)(2,1)S(1)}, u32[]{:S(2)}) copy-start(bf16[256,1024]{0,1:T(8,128)(2,1)S(1)} %copy.141) | copy-start | bytes 1572868
  141.8 15.8 %copy-start.4 = (bf16[256,1,256]{2,0,1:T(8,128)(2,1)S(1)}, bf16[256,1,256]{2,0,1:T(8,128)(2,1)}, u32[]{:S(2)}) copy-start(bf16[256,1,256]{2,0,1:T(8,128)(2,1)} %param.16) | copy-start | bytes 393220
  162.9 0.7 copy-start.7
  165.2 0.7 copy-start.6
  171.1 188.3 %reduce-scatter.5.cloned.1.call-start = ((), (), s32[]{:S(2)}) async-start(), calls=%async_computation.4 | async-start | bytes 18874368 | tf_op jit(solution)/shard_map/reduce_scatter | solution.py:132
  208.0 16.9 %copy-start.10 = (f32[256,16]{0,1:T(8,128)S(1)}, f32[256,16]{0,1:T(8,128)}, u32[]{:S(2)}) copy-start(f32[256,16]{0,1:T(8,128)} %copy-done.9) | copy-start | bytes 49156
  243.4 195.6 %reduce-scatter.3.cloned.1.call-start = ((), (), s32[]{:S(2)}) async-start(), calls=%async_computation.2 | async-start | bytes 5242880 | tf_op jit(solution)/shard_map/reduce_scatter | solution.py:112
Sparse Core Ops, SparseCore 0:
  9.6 83.4 all-gather.5
  106.5 35.2 all-gather.9
  171.2 36.7 all-gather.7
  243.5 115.9 reduce-scatter.4
  362.2 76.7 reduce-scatter.2
where the time goes:
time: 448 us; the launch traced here: 446 us
  waiting for transfers between devices  268 us (60%)
  matrix products  72.6 us (16%)
  other arithmetic  52.1 us (12%)
  local copies, waits for them, and re-layouts  28.5 us (6%)
  between operations  14 us (3%)
  blocking collectives  9.41 us (2%)
    all_gather x1, waiting for transfers between devices, shards(): grad_full = lax.all_gather(grad_out, 'tp', axis=0, tiled=True)  80.8 us
    reduce_scatter x1, waiting for transfers between devices, shards(): lax.psum_scatter(jnp.dot(mixer_bf, out_weight, preferred_element_type=jnp...  75.6 us
    reduce_scatter x1, waiting for transfers between devices, shards(): lax.psum_scatter(lax.dot_general(grad_full, mixer_bf, (((0,), (0,)), ((),...  60.7 us
    all_gather x2, waiting for transfers between devices, prefix(): lax.all_gather(part.astype(kind), axis)  50.1 us
    select_n x16, other arithmetic, step(): return jax.tree.map(lambda a, b: jnp.where(reached, a, b), new, before)  20.6 us
    dot_general x3, matrix products, block_ssd(): inside = jnp.einsum('gkts,sgkp->tgkp', mixing, seq_in, precision=HIGHEST)  16.8 us
    dot_general x1, matrix products, shards(): jnp.dot(mixer_bf, out_weight, preferred_element_type=jnp.float32)  13.4 us
    dot_general x1, matrix products, shards(): lax.dot_general(grad_full, mixer_bf, (((0,), (0,)), ((), ())), preferred_...  12.6 us
  transfers between devices with their start and end apart: 5, of which 5 were waited for; matrix products, arithmetic and copies ran while one was open for 17% of the time, Pallas kernels for 0%

commit v1 on v0

v1 whole, which is shorter than its diff:
```python
import functools
import jax
import jax.numpy as jnp
from jax import lax
from jax.experimental import pallas as pl
from jax.experimental.pallas import tpu as pltpu
from jax.sharding import PartitionSpec as P

F32 = jnp.float32
BF16 = jnp.bfloat16
HIGHEST = lax.Precision.HIGHEST
MASKED = -1e30


def dot(a, b, dims, precision=None):
    return lax.dot_general(
        a, b, ((dims[:1], dims[1:]), ((), ())), precision=precision, preferred_element_type=F32
    )


def spread(cols, pair, width):
    lane = lax.broadcasted_iota(jnp.int32, (1, width), 1)
    first, second = cols[:, 2 * pair : 2 * pair + 1], cols[:, 2 * pair + 1 : 2 * pair + 2]
    return jnp.where(lane < width // 2, first, second)


def triangle(rows):
    down = lax.broadcasted_iota(jnp.int32, (rows, rows), 0)
    across = lax.broadcasted_iota(jnp.int32, (rows, rows), 1)
    return down >= across


def prepare_kernel(
    x_ref, dt_ref, b_ref, bias_ref, rate_ref, docc_ref, docr_ref,
    step_ref, stept_ref, cum_ref, cumt_ref, entry_ref, tail_ref, through_ref, mask_ref, state_ref,
):
    rows, heads = dt_ref.shape
    pair_width = 2 * (x_ref.shape[1] // heads)
    tri = triangle(rows)
    step = jax.nn.softplus(dt_ref[...] + bias_ref[...])
    cum = dot(tri.astype(F32), -step * rate_ref[...], (1, 0), HIGHEST)
    seg_col = jnp.sum(jnp.where(tri, docr_ref[...], 0.0), axis=1, keepdims=True)
    down = lax.broadcasted_iota(jnp.int32, (rows, rows), 0)
    across = lax.broadcasted_iota(jnp.int32, (rows, rows), 1)
    seg_row = jnp.sum(jnp.where(down <= across, docc_ref[...], 0.0), axis=0, keepdims=True)
    total = jnp.sum(docr_ref[...], axis=1, keepdims=True)
    reach = (seg_col == 0.0).astype(F32)
    last = cum[rows - 1 : rows, :]
    entry_ref[...] = jnp.exp(cum) * reach
    tail = jnp.exp(last - cum) * (seg_col == total).astype(F32) * step
    tail_ref[...] = tail
    through_ref[...] = jnp.exp(last) * (total == 0.0).astype(F32)
    step_ref[...] = step
    stept_ref[...] = jnp.transpose(step)
    cum_ref[...] = cum
    cumt_ref[...] = jnp.transpose(cum)
    mask_ref[...] = jnp.where(tri & (seg_col == seg_row), 0.0, MASKED)
    b = b_ref[...]
    for pair in range(heads // 2):
        at = slice(pair * pair_width, (pair + 1) * pair_width)
        scaled = (spread(tail, pair, pair_width) * x_ref[:, at].astype(F32)).astype(BF16)
        state_ref[at, :] = dot(scaled, b, (0, 0)).astype(BF16)


def forward_kernel(
    x_ref, b_ref, c_ref, stept_ref, cum_ref, cumt_ref, entry_ref, skip_ref, mask_ref, carried_ref,
    out_ref,
):
    rows, heads = cum_ref.shape
    width = 2 * (x_ref.shape[1] // heads)
    lane = lax.broadcasted_iota(jnp.int32, (1, width), 1)
    c = c_ref[...]
    scores = dot(c, b_ref[...], (1, 1))
    mask = mask_ref[...]
    for pair in range(heads // 2):
        at = slice(pair * width, (pair + 1) * width)
        x = x_ref[:, at]
        parts = []
        for k in (2 * pair, 2 * pair + 1):
            decay = jnp.exp(cum_ref[:, k : k + 1] - cumt_ref[k : k + 1, :] + mask)
            mixing = decay * stept_ref[k : k + 1, :] * scores
            parts.append(dot(mixing.astype(BF16), x, (1, 0)))
        inside = jnp.where(lane < width // 2, parts[0], parts[1])
        carry = spread(entry_ref, pair, width) * dot(c, carried_ref[at, :], (1, 1))
        out_ref[:, at] = (inside + carry + spread(skip_ref, pair, width) * x.astype(F32)).astype(BF16)


def backward_kernel(
    x_ref, b_ref, c_ref, g_ref, dt_ref, bias_ref, rate_ref, step_ref, stept_ref, cum_ref, cumt_ref,
    entry_ref, tail_ref, through_ref, skip_ref, mask_ref, carried_ref, next_ref,
    dx_ref, ddt_ref, db_ref, dc_ref,
):
    rows, heads = cum_ref.shape
    width = 2 * (x_ref.shape[1] // heads)
    half = width // 2
    lane = lax.broadcasted_iota(jnp.int32, (1, width), 1)
    head_lane = lax.broadcasted_iota(jnp.int32, (1, heads), 1)
    head_row = lax.broadcasted_iota(jnp.int32, (heads, 1), 0)
    c, b = c_ref[...], b_ref[...]
    scores = dot(c, b, (1, 1))
    mask = mask_ref[...]
    dscores = jnp.zeros((rows, rows), F32)
    db = jnp.zeros(b.shape, F32)
    dc = jnp.zeros(c.shape, F32)
    row_sums = jnp.zeros((rows, heads), F32)
    col_sums = jnp.zeros((heads, rows), F32)
    dentry = jnp.zeros((rows, heads), F32)
    dtail = jnp.zeros((rows, heads), F32)
    dthrough = jnp.zeros((1, heads), F32)
    for pair in range(heads // 2):
        at = slice(pair * width, (pair + 1) * width)
        x, g = x_ref[:, at], g_ref[:, at]
        x32, g32 = x.astype(F32), g.astype(F32)
        carried, later = carried_ref[at, :], next_ref[at, :]
        from_carry = dot(c, carried, (1, 1)) * g32
        from_next = dot(b, later, (1, 1))
        tail_pair = spread(tail_ref, pair, width)
        scaled_g = (spread(entry_ref, pair, width) * g32).astype(BF16)
        scaled_x = (tail_pair * x32).astype(BF16)
        dc = dc + dot(scaled_g, carried, (1, 0))
        db = db + dot(scaled_x, later, (1, 0))
        both = carried.astype(F32) * later.astype(F32)
        tail_part = from_next * x32
        parts = []
        for j, k in enumerate((2 * pair, 2 * pair + 1)):
            mine = (lane < half) if j == 0 else (lane >= half)
            decay = jnp.exp(cum_ref[:, k : k + 1] - cumt_ref[k : k + 1, :] + mask)
            stepped = decay * stept_ref[k : k + 1, :]
            mixing = stepped * scores
            dmixing = dot(jnp.where(mine, g, jnp.zeros_like(g)), x, (1, 1))
            parts.append(dot(mixing.astype(BF16), g, (0, 0)))
            dscores = dscores + dmixing * stepped
            product = dmixing * mixing
            row_sums = jnp.where(
                head_lane == k, jnp.sum(product, axis=1, keepdims=True), row_sums
            )
            col_sums = jnp.where(
                head_row == k, jnp.sum(product, axis=0, keepdims=True), col_sums
            )
            dentry = jnp.where(
                head_lane == k,
                jnp.sum(jnp.where(mine, from_carry, 0.0), axis=1, keepdims=True),
                dentry,
            )
            dtail = jnp.where(
                head_lane == k,
                jnp.sum(jnp.where(mine, tail_part, 0.0), axis=1, keepdims=True),
                dtail,
            )
            own = jnp.sum(both[j * half : (j + 1) * half, :], axis=0, keepdims=True)
            dthrough = jnp.where(
                head_lane == k, jnp.sum(own, axis=1, keepdims=True), dthrough
            )
        inside = jnp.where(lane < half, parts[0], parts[1])
        skip = spread(skip_ref, pair, width)
        dx_ref[:, at] = (inside + tail_pair * from_next + skip * g32).astype(BF16)
    ds = dscores.astype(BF16)
    dc_ref[...] = (dc + dot(ds, b, (1, 0))).astype(BF16)
    db_ref[...] = (db + dot(ds, c, (0, 0))).astype(BF16)
    step = step_ref[...]
    tail_flow = dtail * tail_ref[...]
    col = jnp.transpose(col_sums)
    dcum = row_sums - col + dentry * entry_ref[...] - tail_flow
    at_last = jnp.sum(tail_flow, axis=0, keepdims=True) + dthrough * through_ref[...]
    down = lax.broadcasted_iota(jnp.int32, (rows, rows), 0)
    across = lax.broadcasted_iota(jnp.int32, (rows, rows), 1)
    upper = (down <= across).astype(F32)
    dlog = dot(upper, dcum, (1, 0), HIGHEST) + at_last
    dstep = (col + tail_flow) / step - dlog * rate_ref[...]
    ddt_ref[...] = dstep * jax.nn.sigmoid(dt_ref[...] + bias_ref[...])


def call(kernel, outs, *args, name):
    return pl.pallas_call(
        kernel,
        out_shape=[jax.ShapeDtypeStruct(shape, kind) for shape, kind in outs],
        compiler_params=pltpu.CompilerParams(vmem_limit_bytes=48 * 1024 * 1024),
        name=name,
    )(*args)


def swap(value):
    return lax.all_to_all(value, "ctx", 0, 0, tiled=False)


def weight_kernel(count, *refs):
    grads, mixers, out_ref = refs[:count], refs[count : 2 * count], refs[2 * count]
    total = dot(grads[0][...], mixers[0][...], (0, 0))
    for k in range(1, count):
        total = total + dot(grads[k][...], mixers[k][...], (0, 0))
    out_ref[...] = total.astype(BF16)


def shards(
    ssm_input, dt_raw, b_proj, c_proj, dt_bias, decay_rate, skip_gain, doc_start, out_weight, grad_out
):
    rows, inner = ssm_input.shape
    heads = dt_raw.shape[1]
    state = b_proj.shape[2]
    n = lax.axis_size("ctx")
    me = lax.axis_index("ctx")
    grad_full = lax.all_gather(grad_out, "tp", axis=0, tiled=True)

    b = b_proj.reshape(rows, state)
    c = c_proj.reshape(rows, state)
    bias, rate, skip = (v.reshape(1, heads) for v in (dt_bias, decay_rate, skip_gain))
    doc = doc_start.astype(F32)
    th = ((rows, heads), F32)
    ht = ((heads, rows), F32)
    step, stept, cum, cumt, entry, tail, through, mask, local_state = call(
        prepare_kernel,
        [th, ht, th, ht, th, th, ((1, heads), F32), ((rows, rows), F32), ((inner, state), BF16)],
        ssm_input, dt_raw, b, bias, rate, doc.reshape(rows, 1), doc.reshape(1, rows),
        name="prepare",
    )

    share = inner // n
    own_heads = heads // n
    spare = jnp.broadcast_to(
        through.astype(BF16).reshape(n, own_heads, 1), (n, own_heads, 16 // own_heads * state)
    ).reshape(n, 16, state)
    arrived = swap(jnp.concatenate([local_state.reshape(n, share, state), spare], axis=1))
    locals_ = arrived[:, :share].astype(F32)
    throughs = arrived[:, share :: 16 // own_heads, :1].astype(F32)
    factors = jnp.repeat(throughs, share // own_heads, axis=1)
    before = jnp.zeros((share, state), F32)
    befores = []
    for k in range(n):
        befores.append(before.astype(BF16))
        before = factors[k] * before + locals_[k]
    carried = swap(jnp.stack(befores)).reshape(inner, state)

    (mixer_bf,) = call(
        forward_kernel, [((rows, inner), BF16)],
        ssm_input, b, c, stept, cum, cumt, entry, skip, mask, carried, name="forward",
    )
    mixers = [mixer_bf] + [
        lax.ppermute(mixer_bf, "ctx", [(s, s ^ d) for s in range(n)]) for d in range(1, n)
    ]
    layer_out = lax.psum_scatter(
        jnp.dot(mixer_bf, out_weight, preferred_element_type=F32).astype(BF16),
        "tp", scatter_dimension=0, tiled=True,
    )

    grad_mix = dot(grad_full, out_weight, (1, 1)).astype(BF16)
    columns = grad_full.shape[1] // n
    grads = []
    for d in range(n):
        piece = lax.dynamic_slice(grad_full, (0, (me ^ d) * columns), (rows, columns))
        grads.append(piece if d == 0 else lax.ppermute(piece, "ctx", [(s, s ^ d) for s in range(n)]))

    scaled = (
        grad_mix.astype(F32).reshape(rows, heads, -1) * entry[:, :, None]
    ).astype(BF16).reshape(rows, inner)
    local_grad = dot(scaled, c, (0, 0)).astype(BF16)
    locals_ = swap(local_grad.reshape(n, share, state)).astype(F32)
    after = jnp.zeros((share, state), F32)
    afters = [None] * n
    for k in reversed(range(n)):
        afters[k] = after.astype(BF16)
        after = factors[k] * after + locals_[k]
    grad_next = swap(jnp.stack(afters)).reshape(inner, state)

    dx, ddt, db, dc = call(
        backward_kernel,
        [((rows, inner), BF16), th, ((rows, state), BF16), ((rows, state), BF16)],
        ssm_input, b, c, grad_mix, dt_raw, bias, rate, step, stept, cum, cumt,
        entry, tail, through, skip, mask, carried, grad_next, name="backward",
    )
    tile = 256
    weight_grad = pl.pallas_call(
        functools.partial(weight_kernel, n),
        grid=(columns // tile,),
        in_specs=[pl.BlockSpec((rows, tile), lambda i: (0, i))] * n
        + [pl.BlockSpec((rows, inner), lambda i: (0, 0))] * n,
        out_specs=pl.BlockSpec((tile, inner), lambda i: (i, 0)),
        out_shape=jax.ShapeDtypeStruct((columns, inner), BF16),
        compiler_params=pltpu.CompilerParams(vmem_limit_bytes=48 * 1024 * 1024),
        name="weight_grad",
    )(*grads, *mixers)
    return (
        layer_out, dx, ddt, db.reshape(rows, 1, state), dc.reshape(rows, 1, state), weight_grad,
    )


def solution(mesh):
    in_specs = (
        P("ctx", "tp"), P("ctx", "tp"), P("ctx", "tp", None), P("ctx", "tp", None),
        P("tp"), P("tp"), P("tp"), P("ctx"), P("tp", None), P(("ctx", "tp"), None),
    )
    out_specs = (
        P(("ctx", "tp"), None), P("ctx", "tp"), P("ctx", "tp"),
        P("ctx", "tp", None), P("ctx", "tp", None), P("ctx", "tp"),
    )
    return jax.shard_map(shards, mesh=mesh, in_specs=in_specs, out_specs=out_specs, check_vma=False)
```

time: 448 us -> 287 us (0.64)
  waiting for transfers between devices: 268 us -> 127 us
  matrix products: 72.6 us -> 25.8 us
  other arithmetic: 52.1 us -> 8.51 us
  blocking collectives: 9.41 us -> 40.8 us
  starting transfers between devices: 0.6 us -> 21.6 us
  Pallas kernels: 0 us -> 20.7 us
    reduce_scatter x2 -> x1, waiting for transfers between devices: 136 us -> 0.01 us  [shards(): lax.psum_scatter(jnp.dot(mixer_bf, out_weight, preferred_element_type=F32...]
    ppermute x0 -> x14, waiting for transfers between devices: none -> 52.5 us  [the longest x7 39.2 us: shards(): lax.ppermute(piece, 'ctx', [(s, s ^ d) for s in range(n)])]
    all_gather x2 -> x0, waiting for transfers between devices: 50.1 us -> none  [prefix(): lax.all_gather(part.astype(kind), axis)]
    dot_general x15 -> x3, matrix products: 72.6 us -> 25.8 us  [the longest x2 14 us: dot(): lax.dot_general(a, b, ((dims[:1], dims[1:]), ((), ())), precision=precisi...]
    all_to_all x0 -> x2, blocking collectives: none -> 40.8 us  [swap(): return lax.all_to_all(value, 'ctx', 0, 0, tiled=False)]
    all_gather x1, waiting for transfers between devices: 80.8 us -> 56.5 us  [shards(): grad_full = lax.all_gather(grad_out, 'tp', axis=0, tiled=True)]
    pallas_call x0 -> x4, Pallas kernels: none -> 20.7 us  [the longest x3 12.2 us: call(): pl.pallas_call(kernel, out_shape=[jax.ShapeDtypeStruct(shape, kind) for s...]
    select_n x16 -> x0, other arithmetic: 20.6 us -> none  [step(): return jax.tree.map(lambda a, b: jnp.where(reached, a, b), new, before)]
  transfers between devices with their start and end apart: 5 -> 18, of which waited for: 5 -> 9; matrix products, arithmetic and copies ran while one was open for 17% -> 5% of each run, Pallas kernels for 0% -> 7%
where the time goes in v1:
time: 287 us; the launch traced here: 286 us
  waiting for transfers between devices  127 us (44%)
  blocking collectives  40.8 us (14%)
  local copies, waits for them, and re-layouts  27.3 us (10%)
  matrix products  25.8 us (9%)
  starting transfers between devices  21.6 us (8%)
  Pallas kernels  20.7 us (7%)
  between operations  14.5 us (5%)
  other arithmetic  8.51 us (3%)
    all_gather x1, waiting for transfers between devices, shards(): grad_full = lax.all_gather(grad_out, 'tp', axis=0, tiled=True)  56.5 us
    all_to_all x2, blocking collectives, swap(): return lax.all_to_all(value, 'ctx', 0, 0, tiled=False)  40.8 us
    ppermute x7, waiting for transfers between devices, shards(): lax.ppermute(piece, 'ctx', [(s, s ^ d) for s in range(n)])  39.2 us
    unnamed x94, local copies, waits for them, and re-layouts  21.4 us
    all_to_all x2, waiting for transfers between devices, swap(): return lax.all_to_all(value, 'ctx', 0, 0, tiled=False)  17.2 us
    dot_general x2, matrix products, dot(): lax.dot_general(a, b, ((dims[:1], dims[1:]), ((), ())), precision=precisi...  14 us
    ppermute x7, waiting for transfers between devices, shards(): lax.ppermute(mixer_bf, 'ctx', [(s, s ^ d) for s in range(n)])  13.3 us
    pallas_call x3, Pallas kernels, call(): pl.pallas_call(kernel, out_shape=[jax.ShapeDtypeStruct(shape, kind) for s...  12.2 us
  transfers between devices with their start and end apart: 18, of which 9 were waited for; matrix products, arithmetic and copies ran while one was open for 5% of the time, Pallas kernels for 7%

profile of v1, /device:TPU:0, one launch (start us, length us, event | category | flops | bytes accessed | tf_op | source)
XLA Modules:
  0.0 286.2 jit_solution(15693116351514350403)
XLA Ops:
  12.8 1.8 prepare.1
  17.1 5.2 %all-to-all-start = ((bf16[8,144,256]{2,1,0:T(8,128)(2,1)}), bf16[8,144,256]{2,1,0:T(8,128)(2,1)S(1)}, u32[]{:S(2)}, u32[]{:S(2)}) async-start(bf16[8,144,256]{2,1,0:T(8,128)(2,1)} %pad_maximum_fusion), calls=%async_computation | async-start | bytes 1179648 | tf_op jit(solution)/shard_map/all_to_all | solution.py:183
  22.5 1.3 copy.42
  23.8 9.0 %all-to-all-done = bf16[8,144,256]{2,1,0:T(8,128)(2,1)S(1)} async-done(((bf16[8,144,256]{2,1,0:T(8,128)(2,1)}), bf16[8,144,256]{2,1,0:T(8,128)(2,1)S(1)}, u32[]{:S(2)}, u32[]{:S(2)}) %all-to-all-start) | async-done | bytes 589856 | tf_op jit(solution)/shard_map/all_to_all | solution.py:183
  34.3 1.1 slice_convert_fusion
  36.6 56.5 %all-gather.2.cloned.1.call-done = bf16[256,8192]{1,0:T(8,128)(2,1)} async-done(((bf16[64,8192]{1,0:T(8,128)(2,1)}), bf16[256,8192]{1,0:T(8,128)(2,1)}) %all-gather.2.cloned.1.call-update) | async-done | bytes 4194320 | tf_op jit(solution)/shard_map/all_gather | solution.py:202
  93.1 11.6 %convolution_convert_fusion.2.g_ref = bf16[256,1024]{1,0:T(8,128)(2,1)S(1)} fusion(bf16[256,8192]{1,0:T(8,128)(2,1)} %all-gather.2.cloned.1.call-done, bf16[1024,8192]{1,0:T(8,128)(2,1)} %param.18), kind=kOutput, calls=%fused_computation.2 | convolution fusion | flops 4295229440 | bytes 21495808 | tf_op jit(solution)/shard_map/dot_general | solution.py:16
  104.6 2.4 convolution_convert_fusion.1
  107.1 4.3 %all-to-all-start.2 = ((bf16[8,128,256]{2,1,0:T(8,128)(2,1)}), bf16[8,128,256]{2,1,0:T(8,128)(2,1)}, u32[]{:S(2)}, u32[]{:S(2)}) async-start(bf16[8,128,256]{2,1,0:T(8,128)(2,1)} %bitcast.38), calls=%async_computation.3 | async-start | bytes 1048576 | tf_op jit(solution)/shard_map/all_to_all | solution.py:183
  112.8 8.3 %all-to-all-done.2 = bf16[8,128,256]{2,1,0:T(8,128)(2,1)} async-done(((bf16[8,128,256]{2,1,0:T(8,128)(2,1)}), bf16[8,128,256]{2,1,0:T(8,128)(2,1)}, u32[]{:S(2)}, u32[]{:S(2)}) %all-to-all-start.2) | async-done | bytes 524320 | tf_op jit(solution)/shard_map/all_to_all | solution.py:183
  121.1 1.1 convert_element_type.103
  124.0 13.1 %all_to_all.20 = bf16[8,128,256]{2,1,0:T(8,128)(2,1)S(1)} all-to-all(bf16[8,128,256]{2,1,0:T(8,128)(2,1)} %get-tuple-element.84), channel_id=1, replica_groups=mesh['ctx'=8,'tp'=4] {'ctx'}, dimensions={0} | all-to-all | bytes 1048576 | tf_op jit(solution)/shard_map/all_to_all | solution.py:183
  137.2 1.7 forward.1.refs_8_
  138.9 11.9 %convolution_convert_fusion = bf16[256,8192]{1,0:T(8,128)(2,1)} fusion(bf16[256,1024]{1,0:T(8,128)(2,1)S(1)} %forward.1.refs_8_, bf16[1024,8192]{1,0:T(8,128)(2,1)} %param.18), kind=kOutput, calls=%fused_computation | convolution fusion | flops 4297064448 | bytes 21495808 | tf_op jit(solution)/shard_map/dot_general | solution.py:241
  151.0 2.7 constant_dynamic-slice_fusion
  153.8 1.7 collective-permute-start.5
  155.5 1.2 collective-permute-start.4
  156.7 1.5 collective-permute-start.3
  158.2 10.7 %collective-permute-done.6.refs_7_ = bf16[256,1024]{1,0:T(8,128)(2,1)S(1)} collective-permute-done((bf16[256,1024]{1,0:T(8,128)(2,1)S(1)}, bf16[256,1024]{1,0:T(8,128)(2,1)S(1)}, u32[]{:S(2)}, u32[]{:S(2)}) %collective-permute-start.6) | collective-permute-done | bytes 524320 | tf_op jit(solution)/shard_map/ppermute | solution.py:250
  170.2 8.8 %collective-permute-done.5.refs_6_ = bf16[256,1024]{1,0:T(8,128)(2,1)S(1)} collective-permute-done((bf16[256,1024]{1,0:T(8,128)(2,1)S(1)}, bf16[256,1024]{1,0:T(8,128)(2,1)S(1)}, u32[]{:S(2)}, u32[]{:S(2)}) %collective-permute-start.5) | collective-permute-done | bytes 524320 | tf_op jit(solution)/shard_map/ppermute | solution.py:250
  180.7 9.9 %collective-permute-done.4.refs_5_ = bf16[256,1024]{1,0:T(8,128)(2,1)S(1)} collective-permute-done((bf16[256,1024]{1,0:T(8,128)(2,1)S(1)}, bf16[256,1024]{1,0:T(8,128)(2,1)S(1)}, u32[]{:S(2)}, u32[]{:S(2)}) %collective-permute-start.4) | collective-permute-done | bytes 524320 | tf_op jit(solution)/shard_map/ppermute | solution.py:250
  191.5 1.2 collective-permute-start.13
  192.6 9.9 %collective-permute-done.3.refs_4_ = bf16[256,1024]{1,0:T(8,128)(2,1)S(1)} collective-permute-done((bf16[256,1024]{1,0:T(8,128)(2,1)S(1)}, bf16[256,1024]{1,0:T(8,128)(2,1)S(1)}, u32[]{:S(2)}, u32[]{:S(2)}) %collective-permute-start.3) | collective-permute-done | bytes 524320 | tf_op jit(solution)/shard_map/ppermute | solution.py:250
  208.9 1.3 collective-permute-start.9
  210.2 3.7 %collective-permute-done.13.refs_15_ = bf16[256,1024]{1,0:T(8,128)(2,1)S(1)} collective-permute-done((bf16[256,1024]{1,0:T(8,128)(2,1)S(1)}, bf16[256,1024]{1,0:T(8,128)(2,1)S(1)}, u32[]{:S(2)}, u32[]{:S(2)}) %collective-permute-start.13) | collective-permute-done | bytes 524320 | tf_op jit(solution)/shard_map/ppermute | solution.py:238
  214.4 9.6 %collective-permute-done.12.refs_14_ = bf16[256,1024]{1,0:T(8,128)(2,1)S(1)} collective-permute-done((bf16[256,1024]{1,0:T(8,128)(2,1)S(1)}, bf16[256,1024]{1,0:T(8,128)(2,1)S(1)}, u32[]{:S(2)}, u32[]{:S(2)}) %collective-permute-start.12) | collective-permute-done | bytes 524320 | tf_op jit(solution)/shard_map/ppermute | solution.py:238
  224.9 27.7 %all_to_all.21 = bf16[8,128,256]{2,1,0:T(8,128)(2,1)S(1)} all-to-all(bf16[8,128,256]{2,1,0:T(8,128)(2,1)S(1)} %constant_dynamic-update-slice_fusion.1), channel_id=1, replica_groups=mesh['ctx'=8,'tp'=4] {'ctx'}, dimensions={0} | all-to-all | bytes 1048576 | tf_op jit(solution)/shard_map/all_to_all | solution.py:183
  252.7 8.7 %backward.1 = (bf16[256,1024]{1,0:T(8,128)(2,1)}, f32[256,16]{1,0:T(8,128)S(1)}, bf16[256,256]{1,0:T(8,128)(2,1)}, bf16[256,256]{1,0:T(8,128)(2,1)}) custom-call(bf16[256,1024]{1,0:T(8,128)(2,1)S(1)} %copy-done.1, bf16[256,256]{1,0:T(8,128)(2,1)S(1)} %bitcast.25, bf16[256,256]{1,0:T(8,128)(2,1)S(1)} %bitcast.27, ...), custom_call_target="tpu_custom_call" | custom-call | tf_op jit(solution)/shard_map/backward/pallas_call | solution.py:174
  262.0 1.6 copy.44
  265.7 1.0 copy-done.10
  266.8 1.0 copy-done.12
  270.9 8.5 %weight_grad.1 = bf16[1024,1024]{1,0:T(8,128)(2,1)} custom-call(bf16[256,1024]{1,0:T(8,128)(2,1)S(1)} %get-tuple-element.81.refs_0_, bf16[256,1024]{1,0:T(8,128)(2,1)S(1)} %copy-done.18, bf16[256,1024]{1,0:T(8,128)(2,1)S(1)} %copy-done.16, bf16[256,1024]{1,0:T(8,128)(2,1)S(1)} %copy-done.14, bf16[256,1024]{1,0:T(8,128)(2,1)S(1)} %copy-done.12, ...), custom_call_target="tpu_custom_call" | custom-call | tf_op jit(solution)/shard_map/weight_grad/pallas_call | solution.py:271
  (154 shorter events, 31.9 us)
Async XLA Ops:
  7.2 85.9 %all-gather.2.cloned.1.call-start = ((), (), s32[]{:S(2)}) async-start(), calls=%async_computation.6 | async-start | bytes 5242880 | tf_op jit(solution)/shard_map/all_gather | solution.py:202
  15.9 121.3 %copy-start.24 = (f32[16,256]{1,0:T(8,128)}, f32[16,256]{1,0:T(8,128)S(1)}, u32[]{:S(2)}) copy-start(f32[16,256]{1,0:T(8,128)S(1)} %get-tuple-element.21.cumt_ref) | copy-start | bytes 49156
  17.1 15.6 %all-to-all-start = ((bf16[8,144,256]{2,1,0:T(8,128)(2,1)}), bf16[8,144,256]{2,1,0:T(8,128)(2,1)S(1)}, u32[]{:S(2)}, u32[]{:S(2)}) async-start(bf16[8,144,256]{2,1,0:T(8,128)(2,1)} %pad_maximum_fusion), calls=%async_computation | async-start | bytes 1179648 | tf_op jit(solution)/shard_map/all_to_all | solution.py:183
  33.2 89.0 %copy-start.43 = (f32[128]{0:T(128)}, f32[128]{0:T(128)S(1)}, u32[]{:S(2)}) copy-start(f32[128]{0:T(128)S(1)} %mul.211) | copy-start | bytes 1540
  36.6 68.1 %copy-start.4 = (bf16[256,1,256]{2,0,1:T(8,128)(2,1)S(1)}, bf16[256,1,256]{2,0,1:T(8,128)(2,1)}, u32[]{:S(2)}) copy-start(bf16[256,1,256]{2,0,1:T(8,128)(2,1)} %param.13) | copy-start | bytes 393220
  107.1 14.0 %all-to-all-start.2 = ((bf16[8,128,256]{2,1,0:T(8,128)(2,1)}), bf16[8,128,256]{2,1,0:T(8,128)(2,1)}, u32[]{:S(2)}, u32[]{:S(2)}) async-start(bf16[8,128,256]{2,1,0:T(8,128)(2,1)} %bitcast.38), calls=%async_computation.3 | async-start | bytes 1048576 | tf_op jit(solution)/shard_map/all_to_all | solution.py:183
  111.3 168.0 %reduce-scatter.2.cloned.1.call-start = ((), (), s32[]{:S(2)}) async-start(), calls=%async_computation.5 | async-start | bytes 5242880 | tf_op jit(solution)/shard_map/reduce_scatter | solution.py:240
  150.9 53.1 %copy-start.37 = (f32[1,128,256]{2,1,0:T(8,128)S(1)}, f32[1,128,256]{2,1,0:T(8,128)}, u32[]{:S(2)}) copy-start(f32[1,128,256]{2,1,0:T(8,128)} %copy-done.36) | copy-start | bytes 393220
  150.9 53.1 %copy-start.40 = (bf16[8,128,256]{2,1,0:T(8,128)(2,1)S(1)}, bf16[8,128,256]{2,1,0:T(8,128)(2,1)}, u32[]{:S(2)}) copy-start(bf16[8,128,256]{2,1,0:T(8,128)(2,1)} %copy-done.39) | copy-start | bytes 1572868
  150.9 53.1 %copy-start.44 = (f32[128]{0:T(128)S(1)}, f32[128]{0:T(128)}, u32[]{:S(2)}) copy-start(f32[128]{0:T(128)} %copy-done.43) | copy-start | bytes 1540
  150.9 101.7 %copy-start.20 = (f32[256,16]{1,0:T(8,128)S(1)}, f32[256,16]{1,0:T(8,128)}, u32[]{:S(2)}) copy-start(f32[256,16]{1,0:T(8,128)} %copy-done.19) | copy-start | bytes 49156
  150.9 101.7 %copy-start.22 = (f32[256,16]{1,0:T(8,128)S(1)}, f32[256,16]{1,0:T(8,128)}, u32[]{:S(2)}) copy-start(f32[256,16]{1,0:T(8,128)} %copy-done.21) | copy-start | bytes 49156
  150.9 101.7 %copy-start.25 = (f32[16,256]{1,0:T(8,128)S(1)}, f32[16,256]{1,0:T(8,128)}, u32[]{:S(2)}) copy-start(f32[16,256]{1,0:T(8,128)} %copy-done.24) | copy-start | bytes 49156
  150.9 101.7 %copy-start.27 = (f32[16]{0:T(128)S(1)}, f32[16]{0:T(128)}, u32[]{:S(2)}) copy-start(f32[16]{0:T(128)} %param.14) | copy-start | bytes 196
  151.0 101.7 %copy-start.29 = (f32[16]{0:T(128)S(1)}, f32[16]{0:T(128)}, u32[]{:S(2)}) copy-start(f32[16]{0:T(128)} %param.15) | copy-start | bytes 196
  151.0 101.7 %copy-start.31 = (f32[16]{0:T(128)S(1)}, f32[16]{0:T(128)}, u32[]{:S(2)}) copy-start(f32[16]{0:T(128)} %param.16) | copy-start | bytes 196
  151.0 101.7 %copy-start.33 = (f32[1,16]{1,0:T(1,128)S(1)}, f32[1,16]{1,0:T(1,128)}, u32[]{:S(2)}) copy-start(f32[1,16]{1,0:T(1,128)} %copy-done.32) | copy-start | bytes 196
  153.7 15.2 %collective-permute-start.6 = (bf16[256,1024]{1,0:T(8,128)(2,1)S(1)}, bf16[256,1024]{1,0:T(8,128)(2,1)S(1)}, u32[]{:S(2)}, u32[]{:S(2)}) collective-permute-start(bf16[256,1024]{1,0:T(8,128)(2,1)S(1)} %get-tuple-element.74), channel_id=1, source_target_pairs={{0,28},{4,24},{8,20},{12,16},{16,12},{20,8},{24,4},{28,0},{1,29},{... | collective-permute-start | bytes 1572872 | tf_op jit(solution)/shard_map/ppermute | solution.py:250
  153.8 25.2 %collective-permute-start.5 = (bf16[256,1024]{1,0:T(8,128)(2,1)S(1)}, bf16[256,1024]{1,0:T(8,128)(2,1)S(1)}, u32[]{:S(2)}, u32[]{:S(2)}) collective-permute-start(bf16[256,1024]{1,0:T(8,128)(2,1)S(1)} %get-tuple-element.75), channel_id=1, source_target_pairs={{0,24},{4,28},{8,16},{12,20},{16,8},{20,12},{24,0},{28,4},{1,25},{... | collective-permute-start | bytes 1572872 | tf_op jit(solution)/shard_map/ppermute | solution.py:250
  155.5 35.1 %collective-permute-start.4 = (bf16[256,1024]{1,0:T(8,128)(2,1)S(1)}, bf16[256,1024]{1,0:T(8,128)(2,1)S(1)}, u32[]{:S(2)}, u32[]{:S(2)}) collective-permute-start(bf16[256,1024]{1,0:T(8,128)(2,1)S(1)} %get-tuple-element.76), channel_id=1, source_target_pairs={{0,20},{4,16},{8,28},{12,24},{16,4},{20,0},{24,12},{28,8},{1,21},{... | collective-permute-start | bytes 1572872 | tf_op jit(solution)/shard_map/ppermute | solution.py:250
  156.7 45.8 %collective-permute-start.3 = (bf16[256,1024]{1,0:T(8,128)(2,1)S(1)}, bf16[256,1024]{1,0:T(8,128)(2,1)S(1)}, u32[]{:S(2)}, u32[]{:S(2)}) collective-permute-start(bf16[256,1024]{1,0:T(8,128)(2,1)S(1)} %get-tuple-element.77), channel_id=1, source_target_pairs={{0,16},{4,20},{8,24},{12,28},{16,0},{20,4},{24,8},{28,12},{1,17},{... | collective-permute-start | bytes 1572872 | tf_op jit(solution)/shard_map/ppermute | solution.py:250
  158.2 46.8 %collective-permute-start.2 = (bf16[256,1024]{1,0:T(8,128)(2,1)S(1)}, bf16[256,1024]{1,0:T(8,128)(2,1)S(1)}, u32[]{:S(2)}, u32[]{:S(2)}) collective-permute-start(bf16[256,1024]{1,0:T(8,128)(2,1)S(1)} %get-tuple-element.78), channel_id=1, source_target_pairs={{0,12},{4,8},{8,4},{12,0},{16,28},{20,24},{24,20},{28,16},{1,13},{... | collective-permute-start | bytes 1572872 | tf_op jit(solution)/shard_map/ppermute | solution.py:250
  169.7 37.0 %collective-permute-start.1 = (bf16[256,1024]{1,0:T(8,128)(2,1)S(1)}, bf16[256,1024]{1,0:T(8,128)(2,1)S(1)}, u32[]{:S(2)}, u32[]{:S(2)}) collective-permute-start(bf16[256,1024]{1,0:T(8,128)(2,1)S(1)} %get-tuple-element.79), channel_id=1, source_target_pairs={{0,8},{4,12},{8,0},{12,4},{16,24},{20,28},{24,16},{28,20},{1,9},{5... | collective-permute-start | bytes 1572872 | tf_op jit(solution)/shard_map/ppermute | solution.py:250
  179.8 28.3 %collective-permute-start = (bf16[256,1024]{1,0:T(8,128)(2,1)S(1)}, bf16[256,1024]{1,0:T(8,128)(2,1)S(1)}, u32[]{:S(2)}, u32[]{:S(2)}) collective-permute-start(bf16[256,1024]{1,0:T(8,128)(2,1)S(1)} %get-tuple-element.80), channel_id=1, source_target_pairs={{0,4},{4,0},{8,12},{12,8},{16,20},{20,16},{24,28},{28,24},{1,5},{5... | collective-permute-start | bytes 1572872 | tf_op jit(solution)/shard_map/ppermute | solution.py:250
  191.5 22.5 %collective-permute-start.13 = (bf16[256,1024]{1,0:T(8,128)(2,1)S(1)}, bf16[256,1024]{1,0:T(8,128)(2,1)S(1)}, u32[]{:S(2)}, u32[]{:S(2)}) collective-permute-start(bf16[256,1024]{1,0:T(8,128)(2,1)S(1)} %forward.1.refs_8_), channel_id=1, source_target_pairs={{0,28},{4,24},{8,20},{12,16},{16,12},{20,8},{24,4},{28,0},{1,29},{... | collective-permute-start | bytes 1572872 | tf_op jit(solution)/shard_map/ppermute | solution.py:238
  203.3 20.7 %collective-permute-start.12 = (bf16[256,1024]{1,0:T(8,128)(2,1)S(1)}, bf16[256,1024]{1,0:T(8,128)(2,1)S(1)}, u32[]{:S(2)}, u32[]{:S(2)}) collective-permute-start(bf16[256,1024]{1,0:T(8,128)(2,1)S(1)} %forward.1.refs_8_), channel_id=1, source_target_pairs={{0,24},{4,28},{8,16},{12,20},{16,8},{20,12},{24,0},{28,4},{1,25},{... | collective-permute-start | bytes 1572872 | tf_op jit(solution)/shard_map/ppermute | solution.py:238
  205.8 57.8 %collective-permute-start.11 = (bf16[256,1024]{1,0:T(8,128)(2,1)S(1)}, bf16[256,1024]{1,0:T(8,128)(2,1)}, u32[]{:S(2)}, u32[]{:S(2)}) collective-permute-start(bf16[256,1024]{1,0:T(8,128)(2,1)S(1)} %forward.1.refs_8_), channel_id=1, source_target_pairs={{0,20},{4,16},{8,28},{12,24},{16,4},{20,0},{24,12},{28,8},{1,21},{... | collective-permute-start | bytes 1572872 | tf_op jit(solution)/shard_map/ppermute | solution.py:238
  207.6 56.0 %collective-permute-start.10 = (bf16[256,1024]{1,0:T(8,128)(2,1)S(1)}, bf16[256,1024]{1,0:T(8,128)(2,1)}, u32[]{:S(2)}, u32[]{:S(2)}) collective-permute-start(bf16[256,1024]{1,0:T(8,128)(2,1)S(1)} %forward.1.refs_8_), channel_id=1, source_target_pairs={{0,16},{4,20},{8,24},{12,28},{16,0},{20,4},{24,8},{28,12},{1,17},{... | collective-permute-start | bytes 1572872 | tf_op jit(solution)/shard_map/ppermute | solution.py:238
  208.9 54.7 %collective-permute-start.9 = (bf16[256,1024]{1,0:T(8,128)(2,1)S(1)}, bf16[256,1024]{1,0:T(8,128)(2,1)}, u32[]{:S(2)}, u32[]{:S(2)}) collective-permute-start(bf16[256,1024]{1,0:T(8,128)(2,1)S(1)} %forward.1.refs_8_), channel_id=1, source_target_pairs={{0,12},{4,8},{8,4},{12,0},{16,28},{20,24},{24,20},{28,16},{1,13},{... | collective-permute-start | bytes 1572872 | tf_op jit(solution)/shard_map/ppermute | solution.py:238
  213.9 47.4 %copy-start.41 = (bf16[256,1024]{1,0:T(8,128)(2,1)}, bf16[256,1024]{1,0:T(8,128)(2,1)S(1)}, u32[]{:S(2)}) copy-start(bf16[256,1024]{1,0:T(8,128)(2,1)S(1)} %collective-permute-done.13.refs_15_) | copy-start | bytes 1572868
  213.9 49.7 %collective-permute-start.8 = (bf16[256,1024]{1,0:T(8,128)(2,1)S(1)}, bf16[256,1024]{1,0:T(8,128)(2,1)}, u32[]{:S(2)}, u32[]{:S(2)}) collective-permute-start(bf16[256,1024]{1,0:T(8,128)(2,1)S(1)} %forward.1.refs_8_), channel_id=1, source_target_pairs={{0,8},{4,12},{8,0},{12,4},{16,24},{20,28},{24,16},{28,20},{1,9},{5... | collective-permute-start | bytes 1572872 | tf_op jit(solution)/shard_map/ppermute | solution.py:238
  224.0 39.6 %collective-permute-start.7 = (bf16[256,1024]{1,0:T(8,128)(2,1)S(1)}, bf16[256,1024]{1,0:T(8,128)(2,1)}, u32[]{:S(2)}, u32[]{:S(2)}) collective-permute-start(bf16[256,1024]{1,0:T(8,128)(2,1)S(1)} %forward.1.refs_8_), channel_id=1, source_target_pairs={{0,4},{4,0},{8,12},{12,8},{16,20},{20,16},{24,28},{28,24},{1,5},{5... | collective-permute-start | bytes 1572872 | tf_op jit(solution)/shard_map/ppermute | solution.py:238
  (31 other events, 210.1 us)
Sparse Core Ops, SparseCore 0:
  9.6 83.4 all-gather.1
  151.0 73.4 reduce-scatter.1

commit v2 on v0

v2 whole, which is shorter than its diff:
```python
import jax
import jax.numpy as jnp
from jax import lax
from jax.experimental import pallas as pl
from jax.experimental.pallas import tpu as pltpu
from jax.sharding import PartitionSpec as P

F32 = jnp.float32
BF16 = jnp.bfloat16
HIGHEST = lax.Precision.HIGHEST
MASKED = -1e30


def dot(a, b, dims, precision=None):
    return lax.dot_general(
        a, b, ((dims[:1], dims[1:]), ((), ())), precision=precision, preferred_element_type=F32
    )


def column(cols, k):
    lane = lax.broadcasted_iota(jnp.int32, (1, cols.shape[1]), 1)
    return jnp.sum(jnp.where(lane == k, cols, 0.0), axis=1, keepdims=True)


def spread(cols, pair, width):
    lane = lax.broadcasted_iota(jnp.int32, (1, width), 1)
    return jnp.where(lane < width // 2, column(cols, 2 * pair), column(cols, 2 * pair + 1))


def triangle(rows):
    down = lax.broadcasted_iota(jnp.int32, (rows, rows), 0)
    across = lax.broadcasted_iota(jnp.int32, (rows, rows), 1)
    return down >= across


MESH = pl.DeviceIdType.MESH


def mixer_kernel(
    x_ref, dt_ref, b_ref, c_ref, bias_ref, rate_ref, skip_ref, docc_ref, docr_ref, grad_ref, w_hbm,
    layer_ref, dx_ref, ddt_ref, db_ref, dc_ref, wgrad_ref,
    w_ref, full_ref, part_ref, hop_ref, mix_ref, cols_ref,
    pay_ref, arr_ref, back_ref, carried_ref, pay2_ref, arr2_ref, back2_ref, next_ref,
    step_ref, stept_ref, cum_ref, cumt_ref, entry_ref, tail_ref, mask_ref, scores_ref,
    gmix_ref, gacc_ref, acc_ref, sums_ref, colsum_ref, dthrough_ref,
    w_sem, ex_send, ex_recv, mix_send, mix_recv, col_send, col_recv,
    ag_send, ag_recv, hop_send, hop_recv,
):
    n, nz = lax.axis_size("ctx"), lax.axis_size("tp")
    i, me = lax.axis_index("ctx"), lax.axis_index("tp")
    rows, heads = dt_ref.shape
    width = 2 * (x_ref.shape[1] // heads)
    half = width // 2
    own = heads // n
    pairs = heads // 2
    block, model = grad_ref.shape
    columns = model // n
    lane = lax.broadcasted_iota(jnp.int32, (1, width), 1)
    head_lane = lax.broadcasted_iota(jnp.int32, (1, heads), 1)
    down = lax.broadcasted_iota(jnp.int32, (rows, rows), 0)
    across = lax.broadcasted_iota(jnp.int32, (rows, rows), 1)

    def remote(src, dst, send, recv, **where):
        return pltpu.make_async_remote_copy(
            src_ref=src, dst_ref=dst, send_sem=send, recv_sem=recv, device_id=where,
            device_id_type=MESH,
        )

    def peer(d):
        return lax.rem(i + d, n)

    barrier = pltpu.get_barrier_semaphore()
    for d in range(1, n):
        pl.semaphore_signal(barrier, inc=1, device_id={"ctx": peer(d)}, device_id_type=MESH)
    for d in range(1, nz):
        pl.semaphore_signal(
            barrier, inc=1, device_id={"tp": lax.rem(me + d, nz)}, device_id_type=MESH
        )
    pl.semaphore_wait(barrier, n + nz - 2)

    def gather_copy(side, b, src):
        to = me + 1 if side == 0 else me - 1
        return remote(src, full_ref.at[b], ag_send.at[side, b], ag_recv.at[b], tp=to)

    @pl.when(me < nz - 1)
    def _():
        gather_copy(0, me, grad_ref).start()

    @pl.when(me > 0)
    def _():
        gather_copy(1, me, grad_ref).start()

    load = pltpu.make_async_copy(w_hbm, w_ref, w_sem)
    load.start()
    full_ref[pl.ds(me, 1)] = grad_ref[...][None]

    def col_copy(b, d):
        at = pl.multiple_of(peer(d) * columns, columns)
        return remote(
            full_ref.at[b, :, pl.ds(at, columns)], cols_ref.at[d, b],
            col_send.at[b, d], col_recv.at[b, d], ctx=peer(d),
        )

    def send_cols(b):
        for d in range(1, n):
            col_copy(b, d).start()

    def gather_step(r):
        left, right = me - 1 - r, me + 1 + r

        @pl.when(left >= 0)
        def _():
            gather_copy(0, left, full_ref.at[left]).wait_recv()

            @pl.when(me < nz - 1)
            def _():
                gather_copy(0, left, full_ref.at[left]).start()

            send_cols(left)

        @pl.when(right <= nz - 1)
        def _():
            gather_copy(1, right, full_ref.at[right]).wait_recv()

            @pl.when(me > 0)
            def _():
                gather_copy(1, right, full_ref.at[right]).start()

            send_cols(right)

    def hop_copy(side, h, b):
        to = me + 1 if side == 0 else me - 1
        return remote(
            part_ref.at[b], hop_ref.at[side, h], hop_send.at[side, h], hop_recv.at[side, h], tp=to
        )

    def hop_block(side, h):
        return nz - 1 - h + me if side == 0 else h - (nz - 1 - me)

    def hop(h):
        for side in range(2):
            b = hop_block(side, h)
            place = me if side == 0 else nz - 1 - me

            @pl.when(place <= h)
            def _():
                if h > 0:

                    @pl.when(place > 0)
                    def _():
                        hop_copy(side, h - 1, b).wait_recv()
                        total = part_ref[pl.ds(b, 1)].astype(F32)
                        total = total + hop_ref[side, h - 1][None].astype(F32)
                        part_ref[pl.ds(b, 1)] = total.astype(BF16)

                hop_copy(side, h, b).start()

    def exchange(which, src, dst):
        copies = []
        for d in range(1, n):
            copy = remote(src(peer(d)), dst, ex_send.at[which, d], ex_recv.at[which, d], ctx=peer(d))
            copy.start()
            copies.append(copy)
        return copies

    def arrived(copies):
        for copy in copies:
            copy.wait_recv()

    tri = down >= across
    step = jax.nn.softplus(dt_ref[...] + bias_ref[...])
    cum = dot(tri.astype(F32), -step * rate_ref[...], (1, 0), HIGHEST)
    seg_col = jnp.sum(jnp.where(tri, docr_ref[...], 0.0), axis=1, keepdims=True)
    seg_row = jnp.sum(jnp.where(down <= across, docc_ref[...], 0.0), axis=0, keepdims=True)
    total_docs = jnp.sum(docr_ref[...], axis=1, keepdims=True)
    last = cum[rows - 1 : rows, :]
    through = jnp.exp(last) * (total_docs == 0.0).astype(F32)
    entry_ref[...] = jnp.exp(cum) * (seg_col == 0.0).astype(F32)
    tail_ref[...] = jnp.exp(last - cum) * (seg_col == total_docs).astype(F32) * step
    step_ref[...] = step
    stept_ref[...] = jnp.transpose(step)
    cum_ref[...] = cum
    cumt_ref[...] = jnp.transpose(cum)
    mask_ref[...] = jnp.where(tri & (seg_col == seg_row), 0.0, MASKED)
    scores_ref[...] = dot(c_ref[...], b_ref[...], (1, 1))

    def lanes(pair):
        return pl.ds(pl.multiple_of(pair * width, width), width)

    @pl.loop(0, pairs)
    def _(pair):
        x = x_ref[:, lanes(pair)].astype(F32)
        scaled = (spread(tail_ref[...], pair, width) * x).astype(BF16)
        state = dot(scaled, b_ref[...], (0, 0)).astype(BF16)
        for j in range(2):
            pay_ref[2 * pair + j, :half] = state[j * half : (j + 1) * half]
            factor = column(through, 2 * pair + j)
            pay_ref[2 * pair + j, half:] = jnp.broadcast_to(factor, (16, state.shape[1])).astype(BF16)

    def share(ref):
        return lambda to: ref.at[pl.ds(to * own, own)]

    moved = exchange(0, share(pay_ref), arr_ref.at[i])
    arr_ref[pl.ds(i, 1)] = pay_ref[pl.ds(i * own, own)][None]
    send_cols(me)
    arrived(moved)

    def factor(k, j):
        return arr_ref[k, j, half:].astype(F32)[:1]

    def scan(order, local_ref, out_ref):
        for j in range(own):
            state = jnp.zeros((half, arr_ref.shape[3]), F32)
            for k in order:
                out_ref[k, j] = state.astype(BF16)
                state = factor(k, j) * state + local_ref[k, j, :half].astype(F32)

    scan(range(n), arr_ref, back_ref)
    moved2 = exchange(1, lambda to: back_ref.at[to], carried_ref.at[pl.ds(i * own, own)])
    carried_ref[pl.ds(i * own, own)] = back_ref[pl.ds(i, 1)][0]
    arrived(moved2)

    def pair_state(ref, pair):
        return ref[pl.ds(2 * pair, 2)].reshape(width, ref.shape[2])

    @pl.loop(0, pairs)
    def _(pair):
        at = lanes(pair)
        x = x_ref[:, at]
        parts = []
        for j in range(2):
            k = 2 * pair + j
            decay = jnp.exp(column(cum_ref[...], k) - cumt_ref[pl.ds(k, 1), :] + mask_ref[...])
            mixing = decay * stept_ref[pl.ds(k, 1), :] * scores_ref[...]
            parts.append(dot(mixing.astype(BF16), x, (1, 0)))
        inside = jnp.where(lane < half, parts[0], parts[1])
        carry = dot(c_ref[...], pair_state(carried_ref, pair), (1, 1))
        carry = spread(entry_ref[...], pair, width) * carry
        skip = spread(skip_ref[...], pair, width)
        mix_ref[0, :, at] = (inside + carry + skip * x.astype(F32)).astype(BF16)

    mix_copies = []
    for d in range(1, n):
        copy = remote(mix_ref.at[0], mix_ref.at[d], mix_send.at[d], mix_recv.at[d], ctx=peer(d))
        copy.start()
        mix_copies.append(copy)

    gather_step(0)
    load.wait()
    tile = 1024

    @pl.loop(0, model // tile)
    def _(t):
        at = pl.ds(pl.multiple_of(t * tile, tile), tile)
        value = dot(mix_ref[0], w_ref[:, at], (1, 0)).astype(BF16)
        part_ref[:, :, at] = value.reshape(nz, block, tile)

    hop(0)
    for r in range(1, nz - 1):
        gather_step(r)
        if r < nz - 2:
            hop(r)

    gacc_ref[...] = jnp.zeros_like(gacc_ref)

    @pl.loop(0, model // tile)
    def _(t):
        at = pl.ds(pl.multiple_of(t * tile, tile), tile)
        g = full_ref[:, :, at].reshape(rows, tile)
        gacc_ref[...] += dot(g, w_ref[:, at], (1, 1))

    gmix_ref[...] = gacc_ref[...].astype(BF16)

    @pl.loop(0, pairs)
    def _(pair):
        g = gmix_ref[:, lanes(pair)].astype(F32)
        scaled = (spread(entry_ref[...], pair, width) * g).astype(BF16)
        state = dot(scaled, c_ref[...], (0, 0)).astype(BF16)
        for j in range(2):
            pay2_ref[2 * pair + j] = state[j * half : (j + 1) * half]

    moved3 = exchange(2, share(pay2_ref), arr2_ref.at[i])
    arr2_ref[pl.ds(i, 1)] = pay2_ref[pl.ds(i * own, own)][None]
    hop(nz - 2)
    arrived(moved3)
    scan(range(n - 1, -1, -1), arr2_ref, back2_ref)
    moved4 = exchange(3, lambda to: back2_ref.at[to], next_ref.at[pl.ds(i * own, own)])
    next_ref[pl.ds(i * own, own)] = back2_ref[pl.ds(i, 1)][0]

    mine = pl.ds(pl.multiple_of(i * columns, columns), columns)
    cols_ref[0] = full_ref[:, :, mine]
    for copy in mix_copies:
        copy.wait_recv()
    for b in range(nz):
        for d in range(1, n):
            col_copy(b, d).wait_recv()
    out_tile = min(256, columns)

    @pl.loop(0, columns // out_tile)
    def _(t):
        at = pl.ds(pl.multiple_of(t * out_tile, out_tile), out_tile)
        total = jnp.zeros((out_tile, mix_ref.shape[2]), F32)
        for d in range(n):
            total = total + dot(cols_ref[d, :, :, at].reshape(rows, out_tile), mix_ref[d], (0, 0))
        wgrad_ref[at, :] = total.astype(BF16)

    arrived(moved4)

    acc_ref[...] = jnp.zeros_like(acc_ref)
    sums_ref[...] = jnp.zeros_like(sums_ref)
    dthrough_ref[...] = jnp.zeros_like(dthrough_ref)

    @pl.loop(0, pairs)
    def _(pair):
        at = lanes(pair)
        x, g = x_ref[:, at], gmix_ref[:, at]
        x32, g32 = x.astype(F32), g.astype(F32)
        carried, later = pair_state(carried_ref, pair), pair_state(next_ref, pair)
        from_carry = dot(c_ref[...], carried, (1, 1)) * g32
        from_next = dot(b_ref[...], later, (1, 1))
        tail_pair = spread(tail_ref[...], pair, width)
        scaled_g = (spread(entry_ref[...], pair, width) * g32).astype(BF16)
        scaled_x = (tail_pair * x32).astype(BF16)
        acc_ref[1] += dot(scaled_x, later, (1, 0))
        acc_ref[2] += dot(scaled_g, carried, (1, 0))
        both = carried.astype(F32) * later.astype(F32)
        tail_part = from_next * x32
        parts = []
        for j in range(2):
            k = 2 * pair + j
            side = (lane < half) if j == 0 else (lane >= half)
            here = head_lane == k
            decay = jnp.exp(column(cum_ref[...], k) - cumt_ref[pl.ds(k, 1), :] + mask_ref[...])
            stepped = decay * stept_ref[pl.ds(k, 1), :]
            mixing = stepped * scores_ref[...]
            dmixing = dot(jnp.where(side, g, jnp.zeros_like(g)), x, (1, 1))
            parts.append(dot(mixing.astype(BF16), g, (0, 0)))
            acc_ref[0] += dmixing * stepped
            product = dmixing * mixing
            colsum_ref[pl.ds(k, 1), :] = jnp.sum(product, axis=0, keepdims=True)
            for slot, value in enumerate((
                product, jnp.where(side, from_carry, 0.0), jnp.where(side, tail_part, 0.0)
            )):
                summed = jnp.sum(value, axis=1, keepdims=True)
                sums_ref[slot] += jnp.where(here, summed, 0.0)
            alone = jnp.sum(both[j * half : (j + 1) * half, :], axis=0, keepdims=True)
            alone = jnp.sum(alone, axis=1, keepdims=True)
            dthrough_ref[...] += jnp.where(here, alone, 0.0)
        inside = jnp.where(lane < half, parts[0], parts[1])
        skip = spread(skip_ref[...], pair, width)
        dx_ref[:, at] = (inside + tail_pair * from_next + skip * g32).astype(BF16)

    ds = acc_ref[0].astype(BF16)
    db_ref[...] = (acc_ref[1] + dot(ds, c_ref[...], (0, 0))).astype(BF16)
    dc_ref[...] = (acc_ref[2] + dot(ds, b_ref[...], (1, 0))).astype(BF16)
    tail_flow = sums_ref[2] * tail_ref[...]
    col = jnp.transpose(colsum_ref[...])
    dcum = sums_ref[0] - col + sums_ref[1] * entry_ref[...] - tail_flow
    at_last = jnp.sum(tail_flow, axis=0, keepdims=True) + dthrough_ref[...] * through
    upper = (down <= across).astype(F32)
    dlog = dot(upper, dcum, (1, 0), HIGHEST) + at_last
    dstep = (col + tail_flow) / step_ref[...] - dlog * rate_ref[...]
    ddt_ref[...] = dstep * jax.nn.sigmoid(dt_ref[...] + bias_ref[...])

    layer_ref[...] = part_ref[pl.ds(me, 1)][0]
    for side in range(2):
        place = me if side == 0 else nz - 1 - me

        @pl.when(place > 0)
        def _():
            hop_copy(side, nz - 2, me).wait_recv()
            total = layer_ref[...].astype(F32) + hop_ref[side, nz - 2].astype(F32)
            layer_ref[...] = total.astype(BF16)

    for copy in moved + moved2 + moved3 + moved4 + mix_copies:
        copy.wait_send()
    for b in range(nz):
        for d in range(1, n):
            col_copy(b, d).wait_send()

        @pl.when((me < nz - 1) & (me >= b))
        def _():
            gather_copy(0, b, full_ref.at[b]).wait_send()

        @pl.when((me > 0) & (me <= b))
        def _():
            gather_copy(1, b, full_ref.at[b]).wait_send()

    for h in range(nz - 1):
        for side in range(2):
            place = me if side == 0 else nz - 1 - me

            @pl.when(place <= h)
            def _():
                hop_copy(side, h, hop_block(side, h)).wait_send()


def shards(
    ssm_input, dt_raw, b_proj, c_proj, dt_bias, decay_rate, skip_gain, doc_start, out_weight, grad_out
):
    rows, inner = ssm_input.shape
    heads = dt_raw.shape[1]
    state = b_proj.shape[2]
    n, nz = lax.axis_size("ctx"), lax.axis_size("tp")
    block, model = grad_out.shape
    columns = model // n
    dim, own = inner // heads, heads // n
    doc = doc_start.astype(F32)
    th, ht = (rows, heads), (heads, rows)
    V = pltpu.VMEM
    dma = pltpu.SemaphoreType.DMA
    vmem = pl.BlockSpec(memory_space=pltpu.VMEM)
    layer_out, dx, ddt, db, dc, weight_grad = pl.pallas_call(
        mixer_kernel,
        out_shape=[
            jax.ShapeDtypeStruct(shape, kind)
            for shape, kind in (
                ((block, model), BF16), ((rows, inner), BF16), (th, F32),
                ((rows, state), BF16), ((rows, state), BF16), ((columns, inner), BF16),
            )
        ],
        in_specs=[vmem] * 10 + [pl.BlockSpec(memory_space=pl.ANY)],
        out_specs=[vmem] * 6,
        scratch_shapes=[
            V((inner, model), BF16), V((nz, block, model), BF16), V((nz, block, model), BF16),
            V((2, nz - 1, block, model), BF16), V((n, rows, inner), BF16),
            V((n, nz, block, columns), BF16),
            V((heads, dim + 16, state), BF16), V((n, own, dim + 16, state), BF16),
            V((n, own, dim, state), BF16), V((heads, dim, state), BF16),
            V((heads, dim, state), BF16), V((n, own, dim, state), BF16),
            V((n, own, dim, state), BF16), V((heads, dim, state), BF16),
            V(th, F32), V(ht, F32), V(th, F32), V(ht, F32), V(th, F32), V(th, F32),
            V((rows, rows), F32), V((rows, rows), F32),
            V((rows, inner), BF16), V((rows, inner), F32), V((3, rows, state), F32),
            V((3,) + th, F32), V(ht, F32), V((1, heads), F32),
            dma, dma((4, n)), dma((4, n)), dma((n,)), dma((n,)), dma((nz, n)), dma((nz, n)),
            dma((2, nz)), dma((nz,)), dma((2, nz)), dma((2, nz)),
        ],
        compiler_params=pltpu.CompilerParams(
            collective_id=0, has_side_effects=True, vmem_limit_bytes=60 * 1024 * 1024
        ),
        name="mixer",
    )(
        ssm_input, dt_raw, b_proj.reshape(rows, state), c_proj.reshape(rows, state),
        dt_bias.reshape(1, heads), decay_rate.reshape(1, heads), skip_gain.reshape(1, heads),
        doc.reshape(rows, 1), doc.reshape(1, rows), grad_out, out_weight,
    )
    return (
        layer_out, dx, ddt, db.reshape(rows, 1, state), dc.reshape(rows, 1, state), weight_grad,
    )


def solution(mesh):
    in_specs = (
        P("ctx", "tp"), P("ctx", "tp"), P("ctx", "tp", None), P("ctx", "tp", None),
        P("tp"), P("tp"), P("tp"), P("ctx"), P("tp", None), P(("ctx", "tp"), None),
    )
    out_specs = (
        P(("ctx", "tp"), None), P("ctx", "tp"), P("ctx", "tp"),
        P("ctx", "tp", None), P("ctx", "tp", None), P("ctx", "tp"),
    )
    return jax.shard_map(shards, mesh=mesh, in_specs=in_specs, out_specs=out_specs, check_vma=False)
```

time: 448 us -> 156 us (0.35)
  waiting for transfers between devices: 268 us -> 0 us
  Pallas kernels: 0 us -> 144 us
  matrix products: 72.6 us -> 0 us
  other arithmetic: 52.1 us -> 0.68 us
  local copies, waits for them, and re-layouts: 28.5 us -> 10.8 us
  between operations: 14 us -> 0.67 us
  blocking collectives: 9.41 us -> 0 us
    pallas_call x0 -> x1, Pallas kernels: none -> 144 us  [shards(): pl.pallas_call(mixer_kernel, out_shape=[jax.ShapeDtypeStruct(shape, kind)...]
    reduce_scatter x2 -> x0, waiting for transfers between devices: 136 us -> none  [the longest x1 75.6 us: shards(): lax.psum_scatter(jnp.dot(mixer_bf, out_weight, preferred_element_type=jnp...]
    all_gather x3 -> x0, waiting for transfers between devices: 131 us -> none  [the longest x1 80.8 us: shards(): grad_full = lax.all_gather(grad_out, 'tp', axis=0, tiled=True)]
    dot_general x15 -> x0, matrix products: 72.6 us -> none  [the longest x3 16.8 us: block_ssd(): inside = jnp.einsum('gkts,sgkp->tgkp', mixing, seq_in, precision=HIGHEST)]
    select_n x16 -> x0, other arithmetic: 20.6 us -> none  [step(): return jax.tree.map(lambda a, b: jnp.where(reached, a, b), new, before)]
    convert_element_type x18 -> x1, other arithmetic: 12.3 us -> 0.68 us  [shards(): doc = doc_start.astype(F32)]
    all_gather x1 -> x0, blocking collectives: 9.41 us -> none  [prefix(): lax.all_gather(part.astype(kind), axis)]
    another operation x8 -> x0, other arithmetic: 6.93 us -> none
  transfers between devices with their start and end apart: 5 -> 0, of which waited for: 5 -> 0; matrix products, arithmetic and copies ran while one was open for 17% -> 0% of each run, Pallas kernels for 0% -> 0%
where the time goes in v2:
time: 156 us
  Pallas kernels  144 us (92%)
  local copies, waits for them, and re-layouts  10.8 us (7%)
    pallas_call x1, Pallas kernels, shards(): pl.pallas_call(mixer_kernel, out_shape=[jax.ShapeDtypeStruct(shape, kind)...  144 us
    unnamed x15, local copies, waits for them, and re-layouts  9.98 us

profile of v2, /device:TPU:0, one launch (start us, length us, event | category | flops | bytes accessed | tf_op | source)
XLA Modules:
  0.0 155.7 jit_solution(17108312467082018251)
XLA Ops:
  0.6 0.7 convert_element_type.3
  1.3 0.0 copy-start.3
  1.3 0.8 copy.19.docc_ref
  2.1 1.5 copy.18.dt_ref
  3.6 0.0 copy-done.3
  3.6 143.6 %mixer.1 = (bf16[64,8192]{1,0:T(8,128)(2,1)}, bf16[256,1024]{1,0:T(8,128)(2,1)}, f32[256,16]{1,0:T(8,128)}, bf16[256,256]{1,0:T(8,128)(2,1)}, bf16[256,256]{1,0:T(8,128)(2,1)}, /*index=5*/bf16[1024,1024]{1,0:T(8,128)(2,1)}) custom-call(bf16[256,1024]{1,0:T(8,128)(2,1)} %x_ref.1, f32[256,16]{1,0:T(8,128)} %copy.18.dt_ref, bf16[256,256]{1,0:T(8,128)(2,1)} %bitcast.9, ...), custom_call_target="tpu_custom_call" | custom-call | tf_op jit(solution)/shard_map/mixer/pallas_call | solution.py:413
  147.2 0.0 copy-start.2
  147.2 0.0 copy-start.1
  147.2 0.0 copy-start
  147.2 1.7 %copy.20 = f32[256,16]{0,1:T(8,128)} copy(f32[256,16]{1,0:T(8,128)} %get-tuple-element.26) | data formatting | bytes 32768
  148.9 2.3 %copy.26 = bf16[64,8192]{1,0:T(8,128)(2,1)} copy(bf16[64,8192]{1,0:T(8,128)(2,1)} %get-tuple-element.36) | data formatting | bytes 2097152
  151.2 1.9 %copy.27 = bf16[256,1024]{1,0:T(8,128)(2,1)} copy(bf16[256,1024]{1,0:T(8,128)(2,1)} %get-tuple-element.37) | data formatting | bytes 1048576
  153.0 0.0 copy-done.2
  153.1 0.7 copy.28
  153.7 0.0 copy-done.1
  153.7 0.7 copy.29
  154.4 0.0 copy-done
  154.4 1.3 copy.30
Async XLA Ops:
  1.3 2.3 %copy-start.3 = (f32[256]{0:T(256)}, f32[256]{0:T(256)S(1)}, u32[]{:S(2)}) copy-start(f32[256]{0:T(256)S(1)} %convert_element_type.3) | copy-start | bytes 3076
  147.2 5.9 %copy-start.2 = (bf16[256,256]{1,0:T(8,128)(2,1)S(1)}, bf16[256,256]{1,0:T(8,128)(2,1)}, u32[]{:S(2)}) copy-start(bf16[256,256]{1,0:T(8,128)(2,1)} %get-tuple-element.15) | copy-start | bytes 393220
  147.2 6.5 %copy-start.1 = (bf16[256,256]{1,0:T(8,128)(2,1)S(1)}, bf16[256,256]{1,0:T(8,128)(2,1)}, u32[]{:S(2)}) copy-start(bf16[256,256]{1,0:T(8,128)(2,1)} %get-tuple-element.16) | copy-start | bytes 393220
  147.2 7.2 %copy-start = (bf16[1024,1024]{1,0:T(8,128)(2,1)S(1)}, bf16[1024,1024]{1,0:T(8,128)(2,1)}, u32[]{:S(2)}) copy-start(bf16[1024,1024]{1,0:T(8,128)(2,1)} %get-tuple-element.41) | copy-start | bytes 6291460

commit v3 on v2

--- a/solution.py
+++ b/solution.py
@@ -37,7 +37,7 @@
 
 
 def mixer_kernel(
-    x_ref, dt_ref, b_ref, c_ref, bias_ref, rate_ref, skip_ref, docc_ref, docr_ref, grad_ref, w_hbm,
+    x_ref, dt_ref, b_ref, c_ref, bias_ref, rate_ref, skip_ref, doc_ref, grad_ref, w_hbm,
     layer_ref, dx_ref, ddt_ref, db_ref, dc_ref, wgrad_ref,
     w_ref, full_ref, part_ref, hop_ref, mix_ref, cols_ref,
     pay_ref, arr_ref, back_ref, carried_ref, pay2_ref, arr2_ref, back2_ref, next_ref,
@@ -48,7 +48,7 @@
 ):
     n, nz = lax.axis_size("ctx"), lax.axis_size("tp")
     i, me = lax.axis_index("ctx"), lax.axis_index("tp")
-    rows, heads = dt_ref.shape
+    heads, rows = dt_ref.shape
     width = 2 * (x_ref.shape[1] // heads)
     half = width // 2
     own = heads // n
@@ -66,8 +66,10 @@
             device_id_type=MESH,
         )
 
+    group, member = i // 2, lax.rem(i, 2)
+
     def peer(d):
-        return lax.rem(i + d, n)
+        return 2 * lax.rem(group + d // 2, n // 2) + (member if d % 2 == 0 else 1 - member)
 
     barrier = pltpu.get_barrier_semaphore()
     for d in range(1, n):
@@ -78,17 +80,28 @@
         )
     pl.semaphore_wait(barrier, n + nz - 2)
 
-    def gather_copy(side, b, src):
+    part_width = model // 2
+
+    def piece(c):
+        return pl.ds(c * part_width, part_width)
+
+    def gather_copy(side, b, c, src=None):
         to = me + 1 if side == 0 else me - 1
-        return remote(src, full_ref.at[b], ag_send.at[side, b], ag_recv.at[b], tp=to)
+        here = full_ref.at[b, :, piece(c)]
+        return remote(
+            here if src is None else src.at[:, piece(c)], here,
+            ag_send.at[side, b, c], ag_recv.at[b, c], tp=to,
+        )
 
     @pl.when(me < nz - 1)
     def _():
-        gather_copy(0, me, grad_ref).start()
+        for c in range(2):
+            gather_copy(0, me, c, grad_ref).start()
 
     @pl.when(me > 0)
     def _():
-        gather_copy(1, me, grad_ref).start()
+        for c in range(2):
+            gather_copy(1, me, c, grad_ref).start()
 
     load = pltpu.make_async_copy(w_hbm, w_ref, w_sem)
     load.start()
@@ -105,39 +118,34 @@
         for d in range(1, n):
             col_copy(b, d).start()
 
-    def gather_step(r):
-        left, right = me - 1 - r, me + 1 + r
-
-        @pl.when(left >= 0)
-        def _():
-            gather_copy(0, left, full_ref.at[left]).wait_recv()
-
-            @pl.when(me < nz - 1)
+    def gather_step(r, c):
+        for side in range(2):
+            b = me - 1 - r if side == 0 else me + 1 + r
+            inside = b >= 0 if side == 0 else b <= nz - 1
+            onward = me < nz - 1 if side == 0 else me > 0
+
+            @pl.when(inside)
             def _():
-                gather_copy(0, left, full_ref.at[left]).start()
-
-            send_cols(left)
-
-        @pl.when(right <= nz - 1)
-        def _():
-            gather_copy(1, right, full_ref.at[right]).wait_recv()
-
-            @pl.when(me > 0)
-            def _():
-                gather_copy(1, right, full_ref.at[right]).start()
-
-            send_cols(right)
-
-    def hop_copy(side, h, b):
+                gather_copy(side, b, c).wait_recv()
+
+                @pl.when(onward)
+                def _():
+                    gather_copy(side, b, c).start()
+
+                if c == 1:
+                    send_cols(b)
+
+    def hop_copy(side, h, c, b):
         to = me + 1 if side == 0 else me - 1
         return remote(
-            part_ref.at[b], hop_ref.at[side, h], hop_send.at[side, h], hop_recv.at[side, h], tp=to
+            part_ref.at[b, :, piece(c)], hop_ref.at[side, h, :, piece(c)],
+            hop_send.at[side, h, c], hop_recv.at[side, h, c], tp=to,
         )
 
     def hop_block(side, h):
         return nz - 1 - h + me if side == 0 else h - (nz - 1 - me)
 
-    def hop(h):
+    def hop(h, c):
         for side in range(2):
             b = hop_block(side, h)
             place = me if side == 0 else nz - 1 - me
@@ -148,12 +156,12 @@
 
                     @pl.when(place > 0)
                     def _():
-                        hop_copy(side, h - 1, b).wait_recv()
-                        total = part_ref[pl.ds(b, 1)].astype(F32)
-                        total = total + hop_ref[side, h - 1][None].astype(F32)
-                        part_ref[pl.ds(b, 1)] = total.astype(BF16)
-
-                hop_copy(side, h, b).start()
+                        hop_copy(side, h - 1, c, b).wait_recv()
+                        total = part_ref[pl.ds(b, 1), :, piece(c)].astype(F32)
+                        total = total + hop_ref[side, h - 1, :, piece(c)][None].astype(F32)
+                        part_ref[pl.ds(b, 1), :, piece(c)] = total.astype(BF16)
+
+                hop_copy(side, h, c, b).start()
 
     def exchange(which, src, dst):
         copies = []
@@ -168,11 +176,14 @@
             copy.wait_recv()
 
     tri = down >= across
-    step = jax.nn.softplus(dt_ref[...] + bias_ref[...])
+    raw = jnp.transpose(dt_ref[...]) + bias_ref[...]
+    doc_row = doc_ref[...].astype(F32)
+    doc_col = jnp.transpose(jnp.broadcast_to(doc_row, (8, rows)))[:, :1]
+    step = jax.nn.softplus(raw)
     cum = dot(tri.astype(F32), -step * rate_ref[...], (1, 0), HIGHEST)
-    seg_col = jnp.sum(jnp.where(tri, docr_ref[...], 0.0), axis=1, keepdims=True)
-    seg_row = jnp.sum(jnp.where(down <= across, docc_ref[...], 0.0), axis=0, keepdims=True)
-    total_docs = jnp.sum(docr_ref[...], axis=1, keepdims=True)
+    seg_col = jnp.sum(jnp.where(tri, doc_row, 0.0), axis=1, keepdims=True)
+    seg_row = jnp.sum(jnp.where(down <= across, doc_col, 0.0), axis=0, keepdims=True)
+    total_docs = jnp.sum(doc_row, axis=1, keepdims=True)
     last = cum[rows - 1 : rows, :]
     through = jnp.exp(last) * (total_docs == 0.0).astype(F32)
     entry_ref[...] = jnp.exp(cum) * (seg_col == 0.0).astype(F32)
@@ -202,7 +213,6 @@
 
     moved = exchange(0, share(pay_ref), arr_ref.at[i])
     arr_ref[pl.ds(i, 1)] = pay_ref[pl.ds(i * own, own)][None]
-    send_cols(me)
     arrived(moved)
 
     def factor(k, j):
@@ -218,6 +228,8 @@
     scan(range(n), arr_ref, back_ref)
     moved2 = exchange(1, lambda to: back_ref.at[to], carried_ref.at[pl.ds(i * own, own)])
     carried_ref[pl.ds(i * own, own)] = back_ref[pl.ds(i, 1)][0]
+    send_cols(me)
+    gather_step(0, 0)
     arrived(moved2)
 
     def pair_state(ref, pair):
@@ -239,37 +251,57 @@
         skip = spread(skip_ref[...], pair, width)
         mix_ref[0, :, at] = (inside + carry + skip * x.astype(F32)).astype(BF16)
 
-    mix_copies = []
-    for d in range(1, n):
-        copy = remote(mix_ref.at[0], mix_ref.at[d], mix_send.at[d], mix_recv.at[d], ctx=peer(d))
-        copy.start()
-        mix_copies.append(copy)
-
-    gather_step(0)
+    def mix_copy(d):
+        return remote(
+            mix_ref.at[0 if d % 2 == 0 else d - 1], mix_ref.at[d], mix_send.at[d], mix_recv.at[d],
+            ctx=peer(d if d % 2 == 0 else 1),
+        )
+
+    mix_copy(1).start()
+    for d in range(2, n, 2):
+        mix_copy(d).start()
+
     load.wait()
     tile = 1024
 
-    @pl.loop(0, model // tile)
-    def _(t):
-        at = pl.ds(pl.multiple_of(t * tile, tile), tile)
-        value = dot(mix_ref[0], w_ref[:, at], (1, 0)).astype(BF16)
-        part_ref[:, :, at] = value.reshape(nz, block, tile)
-
-    hop(0)
+    def layer_part(c):
+        @pl.loop(0, part_width // tile)
+        def _(t):
+            at = pl.ds(pl.multiple_of(c * part_width + t * tile, tile), tile)
+            value = dot(mix_ref[0], w_ref[:, at], (1, 0)).astype(BF16)
+            part_ref[:, :, at] = value.reshape(nz, block, tile)
+
+    layer_part(0)
+    hop(0, 0)
+    gather_step(0, 1)
+    layer_part(1)
+    hop(0, 1)
+
+    final = jnp.where(me < nz // 2, nz - 1, 0)
+    gacc_ref[...] = jnp.zeros_like(gacc_ref)
+
+    def cotangent(blocks):
+        @pl.loop(0, model // tile)
+        def _(t):
+            at = pl.ds(pl.multiple_of(t * tile, tile), tile)
+            g = jnp.concatenate([full_ref[pl.ds(b, 1), :, at][0] for b in blocks], axis=0)
+            value = dot(g, w_ref[:, at], (1, 1))
+            for k, b in enumerate(blocks):
+                gacc_ref[pl.ds(b, 1)] += value[k * block : (k + 1) * block][None]
+
     for r in range(1, nz - 1):
-        gather_step(r)
+        gather_step(r, 0)
+        gather_step(r, 1)
+        if r == nz - 3:
+            for d in range(2, n, 2):
+                mix_copy(d).wait_recv()
+                mix_copy(d + 1).start()
+            cotangent([lax.rem(final + k, nz) for k in range(1, nz)])
+        hop(r, 0)
         if r < nz - 2:
-            hop(r)
-
-    gacc_ref[...] = jnp.zeros_like(gacc_ref)
-
-    @pl.loop(0, model // tile)
-    def _(t):
-        at = pl.ds(pl.multiple_of(t * tile, tile), tile)
-        g = full_ref[:, :, at].reshape(rows, tile)
-        gacc_ref[...] += dot(g, w_ref[:, at], (1, 1))
-
-    gmix_ref[...] = gacc_ref[...].astype(BF16)
+            hop(r, 1)
+    cotangent([final])
+    gmix_ref[...] = gacc_ref[...].reshape(gmix_ref.shape).astype(BF16)
 
     @pl.loop(0, pairs)
     def _(pair):
@@ -281,7 +313,7 @@
 
     moved3 = exchange(2, share(pay2_ref), arr2_ref.at[i])
     arr2_ref[pl.ds(i, 1)] = pay2_ref[pl.ds(i * own, own)][None]
-    hop(nz - 2)
+    hop(nz - 2, 1)
     arrived(moved3)
     scan(range(n - 1, -1, -1), arr2_ref, back2_ref)
     moved4 = exchange(3, lambda to: back2_ref.at[to], next_ref.at[pl.ds(i * own, own)])
@@ -289,8 +321,8 @@
 
     mine = pl.ds(pl.multiple_of(i * columns, columns), columns)
     cols_ref[0] = full_ref[:, :, mine]
-    for copy in mix_copies:
-        copy.wait_recv()
+    for d in range(1, n, 2):
+        mix_copy(d).wait_recv()
     for b in range(nz):
         for d in range(1, n):
             col_copy(b, d).wait_recv()
@@ -360,7 +392,9 @@
     upper = (down <= across).astype(F32)
     dlog = dot(upper, dcum, (1, 0), HIGHEST) + at_last
     dstep = (col + tail_flow) / step_ref[...] - dlog * rate_ref[...]
-    ddt_ref[...] = dstep * jax.nn.sigmoid(dt_ref[...] + bias_ref[...])
+    ddt_ref[...] = jnp.transpose(
+        dstep * jax.nn.sigmoid(jnp.transpose(dt_ref[...]) + bias_ref[...])
+    )
 
     layer_ref[...] = part_ref[pl.ds(me, 1)][0]
     for side in range(2):
@@ -368,23 +402,28 @@
 
         @pl.when(place > 0)
         def _():
-            hop_copy(side, nz - 2, me).wait_recv()
+            for c in range(2):
+                hop_copy(side, nz - 2, c, me).wait_recv()
             total = layer_ref[...].astype(F32) + hop_ref[side, nz - 2].astype(F32)
             layer_ref[...] = total.astype(BF16)
 
-    for copy in moved + moved2 + moved3 + moved4 + mix_copies:
+    for copy in moved + moved2 + moved3 + moved4:
         copy.wait_send()
+    for d in range(1, n):
+        mix_copy(d).wait_send()
     for b in range(nz):
         for d in range(1, n):
             col_copy(b, d).wait_send()
 
         @pl.when((me < nz - 1) & (me >= b))
         def _():
-            gather_copy(0, b, full_ref.at[b]).wait_send()
+            for c in range(2):
+                gather_copy(0, b, c).wait_send()
 
         @pl.when((me > 0) & (me <= b))
         def _():
-            gather_copy(1, b, full_ref.at[b]).wait_send()
+            for c in range(2):
+                gather_copy(1, b, c).wait_send()
 
     for h in range(nz - 1):
         for side in range(2):
@@ -392,7 +431,8 @@
 
             @pl.when(place <= h)
             def _():
-                hop_copy(side, h, hop_block(side, h)).wait_send()
+                for c in range(2):
+                    hop_copy(side, h, c, hop_block(side, h)).wait_send()
 
 
 def shards(
@@ -405,7 +445,6 @@
     block, model = grad_out.shape
     columns = model // n
     dim, own = inner // heads, heads // n
-    doc = doc_start.astype(F32)
     th, ht = (rows, heads), (heads, rows)
     V = pltpu.VMEM
     dma = pltpu.SemaphoreType.DMA
@@ -415,11 +454,11 @@
         out_shape=[
             jax.ShapeDtypeStruct(shape, kind)
             for shape, kind in (
-                ((block, model), BF16), ((rows, inner), BF16), (th, F32),
+                ((block, model), BF16), ((rows, inner), BF16), (ht, F32),
                 ((rows, state), BF16), ((rows, state), BF16), ((columns, inner), BF16),
             )
         ],
-        in_specs=[vmem] * 10 + [pl.BlockSpec(memory_space=pl.ANY)],
+        in_specs=[vmem] * 9 + [pl.BlockSpec(memory_space=pl.ANY)],
         out_specs=[vmem] * 6,
         scratch_shapes=[
             V((inner, model), BF16), V((nz, block, model), BF16), V((nz, block, model), BF16),
@@ -431,22 +470,22 @@
             V((n, own, dim, state), BF16), V((heads, dim, state), BF16),
             V(th, F32), V(ht, F32), V(th, F32), V(ht, F32), V(th, F32), V(th, F32),
             V((rows, rows), F32), V((rows, rows), F32),
-            V((rows, inner), BF16), V((rows, inner), F32), V((3, rows, state), F32),
+            V((rows, inner), BF16), V((nz, block, inner), F32), V((3, rows, state), F32),
             V((3,) + th, F32), V(ht, F32), V((1, heads), F32),
             dma, dma((4, n)), dma((4, n)), dma((n,)), dma((n,)), dma((nz, n)), dma((nz, n)),
-            dma((2, nz)), dma((nz,)), dma((2, nz)), dma((2, nz)),
+            dma((2, nz, 2)), dma((nz, 2)), dma((2, nz, 2)), dma((2, nz, 2)),
         ],
         compiler_params=pltpu.CompilerParams(
             collective_id=0, has_side_effects=True, vmem_limit_bytes=60 * 1024 * 1024
         ),
         name="mixer",
     )(
-        ssm_input, dt_raw, b_proj.reshape(rows, state), c_proj.reshape(rows, state),
+        ssm_input, dt_raw.T, b_proj.reshape(rows, state), c_proj.reshape(rows, state),
         dt_bias.reshape(1, heads), decay_rate.reshape(1, heads), skip_gain.reshape(1, heads),
-        doc.reshape(rows, 1), doc.reshape(1, rows), grad_out, out_weight,
+        doc_start.reshape(1, rows), grad_out, out_weight,
     )
     return (
-        layer_out, dx, ddt, db.reshape(rows, 1, state), dc.reshape(rows, 1, state), weight_grad,
+        layer_out, dx, ddt.T, db.reshape(rows, 1, state), dc.reshape(rows, 1, state), weight_grad,
     )
 
 

time: 156 us -> 128 us (0.82)
  Pallas kernels: 144 us -> 119 us
  local copies, waits for them, and re-layouts: 10.8 us -> 7.53 us
    pallas_call x1, Pallas kernels: 144 us -> 119 us  [shards(): pl.pallas_call(mixer_kernel, out_shape=[jax.ShapeDtypeStruct(shape, kind)...]
    unnamed x15 -> x14, local copies, waits for them, and re-layouts: 9.98 us -> 7.53 us
where the time goes in v3:
time: 128 us; the launch traced here: 127 us
  Pallas kernels  119 us (93%)
  local copies, waits for them, and re-layouts  7.53 us (6%)
    pallas_call x1, Pallas kernels, shards(): pl.pallas_call(mixer_kernel, out_shape=[jax.ShapeDtypeStruct(shape, kind)...  119 us
    unnamed x14, local copies, waits for them, and re-layouts  7.53 us

profile of v3, /device:TPU:0, one launch (start us, length us, event | category | flops | bytes accessed | tf_op | source)
XLA Modules:
  0.0 127.5 jit_solution(1004780144852540264)
XLA Ops:
  0.6 119.3 %mixer.1 = (bf16[64,8192]{1,0:T(8,128)(2,1)}, bf16[256,1024]{1,0:T(8,128)(2,1)}, f32[16,256]{1,0:T(8,128)}, bf16[256,256]{1,0:T(8,128)(2,1)}, bf16[256,256]{1,0:T(8,128)(2,1)}, /*index=5*/bf16[1024,1024]{1,0:T(8,128)(2,1)}) custom-call(bf16[256,1024]{1,0:T(8,128)(2,1)} %x_ref.1, f32[16,256]{1,0:T(8,128)} %bitcast.14, bf16[256,256]{1,0:T(8,128)(2,1)} %bitcast.10, ...), custom_call_target="tpu_custom_call" | custom-call | tf_op jit(solution)/shard_map/mixer/pallas_call | solution.py:452
  119.9 0.0 copy-start.3
  119.9 0.0 copy-start.2
  119.9 0.0 copy-start.1
  119.9 0.0 copy-start
  119.9 2.4 %copy.22 = bf16[64,8192]{1,0:T(8,128)(2,1)} copy(bf16[64,8192]{1,0:T(8,128)(2,1)} %get-tuple-element.24) | data formatting | bytes 2097152
  122.4 1.9 %copy.23 = bf16[256,1024]{1,0:T(8,128)(2,1)} copy(bf16[256,1024]{1,0:T(8,128)(2,1)} %get-tuple-element.25) | data formatting | bytes 1048576
  124.2 0.0 copy-done.3
  124.2 0.6 copy.24
  124.8 0.0 copy-done.2
  124.8 0.7 copy.25
  125.5 0.0 copy-done.1
  125.5 0.7 copy.26
  126.2 0.0 copy-done
  126.2 1.3 %copy.27 = bf16[1024,1024]{1,0:T(8,128)(2,1)} copy(bf16[1024,1024]{1,0:T(8,128)(2,1)S(1)} %copy-done) | data formatting | bytes 4194304
Async XLA Ops:
  119.9 4.3 %copy-start.3 = (f32[16,256]{1,0:T(8,128)S(1)}, f32[16,256]{1,0:T(8,128)}, u32[]{:S(2)}) copy-start(f32[16,256]{1,0:T(8,128)} %get-tuple-element.14) | copy-start | bytes 49156
  119.9 4.9 %copy-start.2 = (bf16[256,256]{1,0:T(8,128)(2,1)S(1)}, bf16[256,256]{1,0:T(8,128)(2,1)}, u32[]{:S(2)}) copy-start(bf16[256,256]{1,0:T(8,128)(2,1)} %get-tuple-element.15) | copy-start | bytes 393220
  119.9 5.6 %copy-start.1 = (bf16[256,256]{1,0:T(8,128)(2,1)S(1)}, bf16[256,256]{1,0:T(8,128)(2,1)}, u32[]{:S(2)}) copy-start(bf16[256,256]{1,0:T(8,128)(2,1)} %get-tuple-element.16) | copy-start | bytes 393220
  119.9 6.2 %copy-start = (bf16[1024,1024]{1,0:T(8,128)(2,1)S(1)}, bf16[1024,1024]{1,0:T(8,128)(2,1)}, u32[]{:S(2)}) copy-start(bf16[1024,1024]{1,0:T(8,128)(2,1)} %get-tuple-element.29) | copy-start | bytes 6291460

commit v4 on v3

--- a/solution.py
+++ b/solution.py
@@ -42,7 +42,7 @@
     w_ref, full_ref, part_ref, hop_ref, mix_ref, cols_ref,
     pay_ref, arr_ref, back_ref, carried_ref, pay2_ref, arr2_ref, back2_ref, next_ref,
     step_ref, stept_ref, cum_ref, cumt_ref, entry_ref, tail_ref, mask_ref, scores_ref,
-    gmix_ref, gacc_ref, acc_ref, sums_ref, colsum_ref, dthrough_ref,
+    gmix_ref, gacc_ref, wacc_ref, dxacc_ref, acc_ref, sums_ref, colsum_ref, dthrough_ref,
     w_sem, ex_send, ex_recv, mix_send, mix_recv, col_send, col_recv,
     ag_send, ag_recv, hop_send, hop_recv,
 ):
@@ -277,6 +277,12 @@
     layer_part(1)
     hop(0, 1)
 
+    inner = x_ref.shape[1]
+    out_tile = min(256, columns)
+
+    def token_rows(b):
+        return pl.ds(pl.multiple_of(b * block, block), block)
+
     final = jnp.where(me < nz // 2, nz - 1, 0)
     gacc_ref[...] = jnp.zeros_like(gacc_ref)
 
@@ -291,15 +297,38 @@
 
     for r in range(1, nz - 1):
         gather_step(r, 0)
+        if r == nz - 2:
+            hop(r, 0)
         gather_step(r, 1)
         if r == nz - 3:
             for d in range(2, n, 2):
                 mix_copy(d).wait_recv()
                 mix_copy(d + 1).start()
             cotangent([lax.rem(final + k, nz) for k in range(1, nz)])
-        hop(r, 0)
         if r < nz - 2:
+            hop(r, 0)
             hop(r, 1)
+        if r == nz - 3:
+            early = [lax.rem(final + k, nz) for k in range(1, nz)]
+            mine = pl.ds(pl.multiple_of(i * columns, columns), columns)
+            for b in early:
+                cols_ref[0, pl.ds(b, 1)] = full_ref[pl.ds(b, 1), :, mine]
+                for d in range(1, n):
+                    col_copy(b, d).wait_recv()
+            for d in range(1, n, 2):
+                mix_copy(d).wait_recv()
+
+            @pl.loop(0, columns // out_tile)
+            def _(t):
+                at = pl.ds(pl.multiple_of(t * out_tile, out_tile), out_tile)
+                total = jnp.zeros((out_tile, inner), F32)
+                for d in range(n):
+                    left = [cols_ref[d, pl.ds(b, 1), :, at][0] for b in early]
+                    right = [mix_ref[d, token_rows(b), :] for b in early]
+                    total = total + dot(
+                        jnp.concatenate(left, axis=0), jnp.concatenate(right, axis=0), (0, 0)
+                    )
+                wacc_ref[at, :] = total
     cotangent([final])
     gmix_ref[...] = gacc_ref[...].reshape(gmix_ref.shape).astype(BF16)
 
@@ -314,29 +343,6 @@
     moved3 = exchange(2, share(pay2_ref), arr2_ref.at[i])
     arr2_ref[pl.ds(i, 1)] = pay2_ref[pl.ds(i * own, own)][None]
     hop(nz - 2, 1)
-    arrived(moved3)
-    scan(range(n - 1, -1, -1), arr2_ref, back2_ref)
-    moved4 = exchange(3, lambda to: back2_ref.at[to], next_ref.at[pl.ds(i * own, own)])
-    next_ref[pl.ds(i * own, own)] = back2_ref[pl.ds(i, 1)][0]
-
-    mine = pl.ds(pl.multiple_of(i * columns, columns), columns)
-    cols_ref[0] = full_ref[:, :, mine]
-    for d in range(1, n, 2):
-        mix_copy(d).wait_recv()
-    for b in range(nz):
-        for d in range(1, n):
-            col_copy(b, d).wait_recv()
-    out_tile = min(256, columns)
-
-    @pl.loop(0, columns // out_tile)
-    def _(t):
-        at = pl.ds(pl.multiple_of(t * out_tile, out_tile), out_tile)
-        total = jnp.zeros((out_tile, mix_ref.shape[2]), F32)
-        for d in range(n):
-            total = total + dot(cols_ref[d, :, :, at].reshape(rows, out_tile), mix_ref[d], (0, 0))
-        wgrad_ref[at, :] = total.astype(BF16)
-
-    arrived(moved4)
 
     acc_ref[...] = jnp.zeros_like(acc_ref)
     sums_ref[...] = jnp.zeros_like(sums_ref)
@@ -346,17 +352,11 @@
     def _(pair):
         at = lanes(pair)
         x, g = x_ref[:, at], gmix_ref[:, at]
-        x32, g32 = x.astype(F32), g.astype(F32)
-        carried, later = pair_state(carried_ref, pair), pair_state(next_ref, pair)
+        g32 = g.astype(F32)
+        carried = pair_state(carried_ref, pair)
         from_carry = dot(c_ref[...], carried, (1, 1)) * g32
-        from_next = dot(b_ref[...], later, (1, 1))
-        tail_pair = spread(tail_ref[...], pair, width)
         scaled_g = (spread(entry_ref[...], pair, width) * g32).astype(BF16)
-        scaled_x = (tail_pair * x32).astype(BF16)
-        acc_ref[1] += dot(scaled_x, later, (1, 0))
         acc_ref[2] += dot(scaled_g, carried, (1, 0))
-        both = carried.astype(F32) * later.astype(F32)
-        tail_part = from_next * x32
         parts = []
         for j in range(2):
             k = 2 * pair + j
@@ -370,17 +370,54 @@
             acc_ref[0] += dmixing * stepped
             product = dmixing * mixing
             colsum_ref[pl.ds(k, 1), :] = jnp.sum(product, axis=0, keepdims=True)
-            for slot, value in enumerate((
-                product, jnp.where(side, from_carry, 0.0), jnp.where(side, tail_part, 0.0)
-            )):
+            for slot, value in enumerate((product, jnp.where(side, from_carry, 0.0))):
                 summed = jnp.sum(value, axis=1, keepdims=True)
                 sums_ref[slot] += jnp.where(here, summed, 0.0)
+        inside = jnp.where(lane < half, parts[0], parts[1])
+        dxacc_ref[:, at] = inside + spread(skip_ref[...], pair, width) * g32
+
+    arrived(moved3)
+    scan(range(n - 1, -1, -1), arr2_ref, back2_ref)
+    moved4 = exchange(3, lambda to: back2_ref.at[to], next_ref.at[pl.ds(i * own, own)])
+    next_ref[pl.ds(i * own, own)] = back2_ref[pl.ds(i, 1)][0]
+
+    cols_ref[0, pl.ds(final, 1)] = full_ref[pl.ds(final, 1), :, mine]
+    for d in range(1, n):
+        col_copy(final, d).wait_recv()
+    staged = w_ref.at[pl.ds(0, columns), pl.ds(0, inner)]
+
+    @pl.loop(0, columns // out_tile)
+    def _(t):
+        at = pl.ds(pl.multiple_of(t * out_tile, out_tile), out_tile)
+        left = [cols_ref[d, pl.ds(final, 1), :, at][0] for d in range(n)]
+        right = [mix_ref[d, token_rows(final), :] for d in range(n)]
+        total = dot(jnp.concatenate(left, axis=0), jnp.concatenate(right, axis=0), (0, 0))
+        w_ref[at, pl.ds(0, inner)] = (wacc_ref[at, :] + total).astype(BF16)
+
+    store = pltpu.make_async_copy(staged, wgrad_ref, w_sem)
+    store.start()
+
+    arrived(moved4)
+
+    @pl.loop(0, pairs)
+    def _(pair):
+        at = lanes(pair)
+        x32 = x_ref[:, at].astype(F32)
+        carried, later = pair_state(carried_ref, pair), pair_state(next_ref, pair)
+        from_next = dot(b_ref[...], later, (1, 1))
+        tail_pair = spread(tail_ref[...], pair, width)
+        acc_ref[1] += dot((tail_pair * x32).astype(BF16), later, (1, 0))
+        both = carried.astype(F32) * later.astype(F32)
+        tail_part = from_next * x32
+        for j in range(2):
+            side = (lane < half) if j == 0 else (lane >= half)
+            here = head_lane == 2 * pair + j
+            summed = jnp.sum(jnp.where(side, tail_part, 0.0), axis=1, keepdims=True)
+            sums_ref[2] += jnp.where(here, summed, 0.0)
             alone = jnp.sum(both[j * half : (j + 1) * half, :], axis=0, keepdims=True)
             alone = jnp.sum(alone, axis=1, keepdims=True)
             dthrough_ref[...] += jnp.where(here, alone, 0.0)
-        inside = jnp.where(lane < half, parts[0], parts[1])
-        skip = spread(skip_ref[...], pair, width)
-        dx_ref[:, at] = (inside + tail_pair * from_next + skip * g32).astype(BF16)
+        dx_ref[:, at] = (dxacc_ref[:, at] + tail_pair * from_next).astype(BF16)
 
     ds = acc_ref[0].astype(BF16)
     db_ref[...] = (acc_ref[1] + dot(ds, c_ref[...], (0, 0))).astype(BF16)
@@ -407,6 +444,8 @@
             total = layer_ref[...].astype(F32) + hop_ref[side, nz - 2].astype(F32)
             layer_ref[...] = total.astype(BF16)
 
+    store.wait()
+
     for copy in moved + moved2 + moved3 + moved4:
         copy.wait_send()
     for d in range(1, n):
@@ -433,6 +472,21 @@
             def _():
                 for c in range(2):
                     hop_copy(side, h, c, hop_block(side, h)).wait_send()
+
+
+def settle_kernel(*refs):
+    sems = refs[12]
+    copies = []
+    for k in range(6):
+        rows = refs[k].shape[0]
+        cuts = 4 if rows % 64 == 0 else 1
+        for cut in range(cuts):
+            at = pl.ds(cut * (rows // cuts), rows // cuts)
+            copies.append(pltpu.make_async_copy(refs[k].at[at], refs[6 + k].at[at], sems.at[k, cut]))
+    for copy in copies:
+        copy.start()
+    for copy in copies:
+        copy.wait()
 
 
 def shards(
@@ -449,7 +503,7 @@
     V = pltpu.VMEM
     dma = pltpu.SemaphoreType.DMA
     vmem = pl.BlockSpec(memory_space=pltpu.VMEM)
-    layer_out, dx, ddt, db, dc, weight_grad = pl.pallas_call(
+    results = pl.pallas_call(
         mixer_kernel,
         out_shape=[
             jax.ShapeDtypeStruct(shape, kind)
@@ -459,7 +513,7 @@
             )
         ],
         in_specs=[vmem] * 9 + [pl.BlockSpec(memory_space=pl.ANY)],
-        out_specs=[vmem] * 6,
+        out_specs=[vmem] * 5 + [pl.BlockSpec(memory_space=pl.ANY)],
         scratch_shapes=[
             V((inner, model), BF16), V((nz, block, model), BF16), V((nz, block, model), BF16),
             V((2, nz - 1, block, model), BF16), V((n, rows, inner), BF16),
@@ -470,7 +524,8 @@
             V((n, own, dim, state), BF16), V((heads, dim, state), BF16),
             V(th, F32), V(ht, F32), V(th, F32), V(ht, F32), V(th, F32), V(th, F32),
             V((rows, rows), F32), V((rows, rows), F32),
-            V((rows, inner), BF16), V((nz, block, inner), F32), V((3, rows, state), F32),
+            V((rows, inner), BF16), V((nz, block, inner), F32), V((columns, inner), F32), V((rows, inner), F32),
+            V((3, rows, state), F32),
             V((3,) + th, F32), V(ht, F32), V((1, heads), F32),
             dma, dma((4, n)), dma((4, n)), dma((n,)), dma((n,)), dma((nz, n)), dma((nz, n)),
             dma((2, nz, 2)), dma((nz, 2)), dma((2, nz, 2)), dma((2, nz, 2)),
@@ -484,6 +539,16 @@
         dt_bias.reshape(1, heads), decay_rate.reshape(1, heads), skip_gain.reshape(1, heads),
         doc_start.reshape(1, rows), grad_out, out_weight,
     )
+    anywhere = pl.BlockSpec(memory_space=pl.ANY)
+    layer_out, dx, ddt, db, dc, weight_grad = pl.pallas_call(
+        settle_kernel,
+        out_shape=[jax.ShapeDtypeStruct(part.shape, part.dtype) for part in results],
+        in_specs=[anywhere] * 6,
+        out_specs=[anywhere] * 6,
+        scratch_shapes=[dma((6, 4))],
+        compiler_params=pltpu.CompilerParams(vmem_limit_bytes=60 * 1024 * 1024),
+        name="settle",
+    )(*results)
     return (
         layer_out, dx, ddt.T, db.reshape(rows, 1, state), dc.reshape(rows, 1, state), weight_grad,
     )

time: 128 us -> 243 us (1.90)
  Pallas kernels: 119 us -> 242 us
  local copies, waits for them, and re-layouts: 7.53 us -> 0 us
    pallas_call x0 -> x1, Pallas kernels: none -> 121 us  [shards(): pl.pallas_call(settle_kernel, out_shape=[jax.ShapeDtypeStruct(part.shape,...]
    unnamed x14 -> x0, local copies, waits for them, and re-layouts: 7.53 us -> none
where the time goes in v4:
time: 243 us
  Pallas kernels  242 us (100%)
    pallas_call x1, Pallas kernels, shards(): pl.pallas_call(mixer_kernel, out_shape=[jax.ShapeDtypeStruct(shape, kind)...  122 us
    pallas_call x1, Pallas kernels, shards(): pl.pallas_call(settle_kernel, out_shape=[jax.ShapeDtypeStruct(part.shape,...  121 us

profile of v4, /device:TPU:0, one launch (start us, length us, event | category | flops | bytes accessed | tf_op | source)
XLA Modules:
  0.0 243.1 jit_solution(7212883956381305657)
XLA Ops:
  0.6 121.5 %mixer.1 = (bf16[64,8192]{1,0:T(8,128)(2,1)}, bf16[256,1024]{1,0:T(8,128)(2,1)}, f32[16,256]{1,0:T(8,128)}, bf16[256,256]{1,0:T(8,128)(2,1)}, bf16[256,256]{1,0:T(8,128)(2,1)}, /*index=5*/bf16[1024,1024]{1,0:T(8,128)(2,1)}) custom-call(bf16[256,1024]{1,0:T(8,128)(2,1)} %x_ref.1, f32[16,256]{1,0:T(8,128)} %bitcast.12, bf16[256,256]{1,0:T(8,128)(2,1)} %bitcast.10, ...), custom_call_target="tpu_custom_call" | custom-call | tf_op jit(solution)/shard_map/mixer/pallas_call | solution.py:506
  122.2 120.9 %settle.1 = (bf16[64,8192]{1,0:T(8,128)(2,1)}, bf16[256,1024]{1,0:T(8,128)(2,1)}, f32[16,256]{1,0:T(8,128)}, bf16[256,256]{1,0:T(8,128)(2,1)}, bf16[256,256]{1,0:T(8,128)(2,1)}, /*index=5*/bf16[1024,1024]{1,0:T(8,128)(2,1)}) custom-call(bf16[64,8192]{1,0:T(8,128)(2,1)} %get-tuple-element.18.refs_0_, bf16[256,1024]{1,0:T(8,128)(2,1)} %get-tuple-element.19.refs_1_, ...), custom_call_target="tpu_custom_call" | custom-call | tf_op jit(solution)/shard_map/settle/pallas_call | solution.py:543

commit v5 on v4

--- a/solution.py
+++ b/solution.py
@@ -85,11 +85,16 @@
     def piece(c):
         return pl.ds(c * part_width, part_width)
 
+    part_rows = block // 2
+
+    def row_piece(c):
+        return pl.ds(c * part_rows, part_rows)
+
     def gather_copy(side, b, c, src=None):
         to = me + 1 if side == 0 else me - 1
-        here = full_ref.at[b, :, piece(c)]
+        here = full_ref.at[b, row_piece(c)]
         return remote(
-            here if src is None else src.at[:, piece(c)], here,
+            here if src is None else src.at[row_piece(c)], here,
             ag_send.at[side, b, c], ag_recv.at[b, c], tp=to,
         )
 
@@ -107,16 +112,16 @@
     load.start()
     full_ref[pl.ds(me, 1)] = grad_ref[...][None]
 
-    def col_copy(b, d):
+    def col_copy(b, c, d):
         at = pl.multiple_of(peer(d) * columns, columns)
         return remote(
-            full_ref.at[b, :, pl.ds(at, columns)], cols_ref.at[d, b],
-            col_send.at[b, d], col_recv.at[b, d], ctx=peer(d),
+            full_ref.at[b, row_piece(c), pl.ds(at, columns)], cols_ref.at[d, b, row_piece(c)],
+            col_send.at[b, c, d], col_recv.at[b, c, d], ctx=peer(d),
         )
 
-    def send_cols(b):
+    def send_cols(b, c):
         for d in range(1, n):
-            col_copy(b, d).start()
+            col_copy(b, c, d).start()
 
     def gather_step(r, c):
         for side in range(2):
@@ -132,8 +137,7 @@
                 def _():
                     gather_copy(side, b, c).start()
 
-                if c == 1:
-                    send_cols(b)
+                send_cols(b, c)
 
     def hop_copy(side, h, c, b):
         to = me + 1 if side == 0 else me - 1
@@ -228,7 +232,8 @@
     scan(range(n), arr_ref, back_ref)
     moved2 = exchange(1, lambda to: back_ref.at[to], carried_ref.at[pl.ds(i * own, own)])
     carried_ref[pl.ds(i * own, own)] = back_ref[pl.ds(i, 1)][0]
-    send_cols(me)
+    send_cols(me, 0)
+    send_cols(me, 1)
     gather_step(0, 0)
     arrived(moved2)
 
@@ -295,40 +300,41 @@
             for k, b in enumerate(blocks):
                 gacc_ref[pl.ds(b, 1)] += value[k * block : (k + 1) * block][None]
 
-    for r in range(1, nz - 1):
+    for r in range(1, nz - 2):
         gather_step(r, 0)
-        if r == nz - 2:
-            hop(r, 0)
+        hop(r, 0)
         gather_step(r, 1)
-        if r == nz - 3:
-            for d in range(2, n, 2):
-                mix_copy(d).wait_recv()
-                mix_copy(d + 1).start()
-            cotangent([lax.rem(final + k, nz) for k in range(1, nz)])
-        if r < nz - 2:
-            hop(r, 0)
-            hop(r, 1)
-        if r == nz - 3:
-            early = [lax.rem(final + k, nz) for k in range(1, nz)]
-            mine = pl.ds(pl.multiple_of(i * columns, columns), columns)
-            for b in early:
-                cols_ref[0, pl.ds(b, 1)] = full_ref[pl.ds(b, 1), :, mine]
-                for d in range(1, n):
-                    col_copy(b, d).wait_recv()
-            for d in range(1, n, 2):
-                mix_copy(d).wait_recv()
-
-            @pl.loop(0, columns // out_tile)
-            def _(t):
-                at = pl.ds(pl.multiple_of(t * out_tile, out_tile), out_tile)
-                total = jnp.zeros((out_tile, inner), F32)
-                for d in range(n):
-                    left = [cols_ref[d, pl.ds(b, 1), :, at][0] for b in early]
-                    right = [mix_ref[d, token_rows(b), :] for b in early]
-                    total = total + dot(
-                        jnp.concatenate(left, axis=0), jnp.concatenate(right, axis=0), (0, 0)
-                    )
-                wacc_ref[at, :] = total
+        hop(r, 1)
+    for d in range(2, n, 2):
+        mix_copy(d).wait_recv()
+        mix_copy(d + 1).start()
+    early = [lax.rem(final + k, nz) for k in range(1, nz)]
+    cotangent(early)
+    gather_step(nz - 2, 0)
+    hop(nz - 2, 0)
+
+    mine = pl.ds(pl.multiple_of(i * columns, columns), columns)
+    for b in early:
+        cols_ref[0, pl.ds(b, 1)] = full_ref[pl.ds(b, 1), :, mine]
+        for d in range(1, n):
+            for c in range(2):
+                col_copy(b, c, d).wait_recv()
+    for d in range(1, n, 2):
+        mix_copy(d).wait_recv()
+
+    @pl.loop(0, columns // out_tile)
+    def _(t):
+        at = pl.ds(pl.multiple_of(t * out_tile, out_tile), out_tile)
+        total = jnp.zeros((out_tile, inner), F32)
+        for d in range(n):
+            left = [cols_ref[d, pl.ds(b, 1), :, at][0] for b in early]
+            right = [mix_ref[d, token_rows(b), :] for b in early]
+            total = total + dot(
+                jnp.concatenate(left, axis=0), jnp.concatenate(right, axis=0), (0, 0)
+            )
+        wacc_ref[at, :] = total
+    hop(nz - 2, 1)
+    gather_step(nz - 2, 1)
     cotangent([final])
     gmix_ref[...] = gacc_ref[...].reshape(gmix_ref.shape).astype(BF16)
 
@@ -342,7 +348,6 @@
 
     moved3 = exchange(2, share(pay2_ref), arr2_ref.at[i])
     arr2_ref[pl.ds(i, 1)] = pay2_ref[pl.ds(i * own, own)][None]
-    hop(nz - 2, 1)
 
     acc_ref[...] = jnp.zeros_like(acc_ref)
     sums_ref[...] = jnp.zeros_like(sums_ref)
@@ -383,7 +388,8 @@
 
     cols_ref[0, pl.ds(final, 1)] = full_ref[pl.ds(final, 1), :, mine]
     for d in range(1, n):
-        col_copy(final, d).wait_recv()
+        for c in range(2):
+            col_copy(final, c, d).wait_recv()
     staged = w_ref.at[pl.ds(0, columns), pl.ds(0, inner)]
 
     @pl.loop(0, columns // out_tile)
@@ -452,7 +458,8 @@
         mix_copy(d).wait_send()
     for b in range(nz):
         for d in range(1, n):
-            col_copy(b, d).wait_send()
+            for c in range(2):
+                col_copy(b, c, d).wait_send()
 
         @pl.when((me < nz - 1) & (me >= b))
         def _():
@@ -527,7 +534,7 @@
             V((rows, inner), BF16), V((nz, block, inner), F32), V((columns, inner), F32), V((rows, inner), F32),
             V((3, rows, state), F32),
             V((3,) + th, F32), V(ht, F32), V((1, heads), F32),
-            dma, dma((4, n)), dma((4, n)), dma((n,)), dma((n,)), dma((nz, n)), dma((nz, n)),
+            dma, dma((4, n)), dma((4, n)), dma((n,)), dma((n,)), dma((nz, 2, n)), dma((nz, 2, n)),
             dma((2, nz, 2)), dma((nz, 2)), dma((2, nz, 2)), dma((2, nz, 2)),
         ],
         compiler_params=pltpu.CompilerParams(
@@ -543,7 +550,7 @@
     layer_out, dx, ddt, db, dc, weight_grad = pl.pallas_call(
         settle_kernel,
         out_shape=[jax.ShapeDtypeStruct(part.shape, part.dtype) for part in results],
-        in_specs=[anywhere] * 6,
+        in_specs=[vmem] * 6,
         out_specs=[anywhere] * 6,
         scratch_shapes=[dma((6, 4))],
         compiler_params=pltpu.CompilerParams(vmem_limit_bytes=60 * 1024 * 1024),

time: 243 us -> 124 us (0.51)
  Pallas kernels: 242 us -> 124 us
    pallas_call x1, Pallas kernels: 121 us -> 4.31 us  [shards(): pl.pallas_call(settle_kernel, out_shape=[jax.ShapeDtypeStruct(part.shape,...]
where the time goes in v5:
time: 124 us
  Pallas kernels  124 us (100%)
    pallas_call x1, Pallas kernels, shards(): pl.pallas_call(mixer_kernel, out_shape=[jax.ShapeDtypeStruct(shape, kind)...  119 us
    pallas_call x1, Pallas kernels, shards(): pl.pallas_call(settle_kernel, out_shape=[jax.ShapeDtypeStruct(part.shape,...  4.31 us

profile of v5, /device:TPU:0, one launch (start us, length us, event | category | flops | bytes accessed | tf_op | source)
XLA Modules:
  0.0 124.3 jit_solution(1085890697273534904)
XLA Ops:
  0.6 119.3 %mixer.1 = (bf16[64,8192]{1,0:T(8,128)(2,1)}, bf16[256,1024]{1,0:T(8,128)(2,1)}, f32[16,256]{1,0:T(8,128)}, bf16[256,256]{1,0:T(8,128)(2,1)}, bf16[256,256]{1,0:T(8,128)(2,1)}, /*index=5*/bf16[1024,1024]{1,0:T(8,128)(2,1)}) custom-call(bf16[256,1024]{1,0:T(8,128)(2,1)} %x_ref.1, f32[16,256]{1,0:T(8,128)} %bitcast.12, bf16[256,256]{1,0:T(8,128)(2,1)} %bitcast.10, ...), custom_call_target="tpu_custom_call" | custom-call | tf_op jit(solution)/shard_map/mixer/pallas_call | solution.py:513
  120.0 4.3 %settle.1 = (bf16[64,8192]{1,0:T(8,128)(2,1)}, bf16[256,1024]{1,0:T(8,128)(2,1)}, f32[16,256]{1,0:T(8,128)}, bf16[256,256]{1,0:T(8,128)(2,1)}, bf16[256,256]{1,0:T(8,128)(2,1)}, /*index=5*/bf16[1024,1024]{1,0:T(8,128)(2,1)}) custom-call(bf16[64,8192]{1,0:T(8,128)(2,1)} %get-tuple-element.18.refs_0_, bf16[256,1024]{1,0:T(8,128)(2,1)} %get-tuple-element.19.refs_1_, ...), custom_call_target="tpu_custom_call" | custom-call | tf_op jit(solution)/shard_map/settle/pallas_call | solution.py:550
